TPU v7x, 32 devices: a whole 2x2x4 slice. The times are simulated.
32 devices in a mesh: dp: 8 (over y, x, core), mp: 4 (over z).
Axes of the slice: x: 2, y: 2, z: 4, core: 2. Of those that a mesh axis runs over, the one named last changes fastest.
Arguments:
- tokens: bfloat16 [2048, 4096], P('dp'), may hold values from -32 to 32
- weights: bfloat16 [4096, 2, 3, 4096], P('dp', None, None, 'mp'), may hold values from -1 to 1
- block_modality: int32 [16], replicated, may hold values from 0 to 1
- doc_ids: int32 [2048], replicated, may hold values from 0 to 15, never falling along the last dimension, each value on 1 to 1024 neighbouring positions
- grad_out: bfloat16 [2048, 4096], P('dp', 'mp'), may hold values from -6 to 6
Outputs:
- attended: bfloat16 [2048, 4096], P('dp', 'mp')
- grad_tokens: bfloat16 [2048, 4096], P('dp', 'mp')
- grad_weights: bfloat16 [4096, 2, 3, 4096], P('dp', None, None, 'mp')
Inputs may be any that keep to these rules, and one draw needn't show every extreme that they name: doc_ids never falls along the sequence; a document is a run of equal ids of at most 1024 tokens, and one document has exactly 1024.
All inputs are finite; a program needn't handle non-finite values.
Results may differ from a plain program's by a relative error of at most 0.025.
Values may be sent and summed in bfloat16 or wider, within the bound.
A program may use at most 192 MiB of HBM per device.

v0:
```python
import jax
import jax.numpy as jnp
from jax import lax
from jax.sharding import PartitionSpec as P

HD = 128
BLOCK = 128
SPAN = 4


def shifted(block, axis, distance):
    devices = range(lax.axis_size(axis))
    route = [(i - distance, i) for i in devices if i - distance in devices]
    return lax.ppermute(block, axis, route)


def select_product(block_rows, modality, text_mat, image_mat, contract):
    contraction = (((1,), (contract,)), ((), ()))
    return lax.cond(
        modality == 0,
        lambda: lax.dot_general(
            block_rows, text_mat, contraction, preferred_element_type=jnp.float32
        ),
        lambda: lax.dot_general(
            block_rows, image_mat, contraction, preferred_element_type=jnp.float32
        ),
    )


def blockwise(row_data, modalities, text_mat, image_mat, contract):
    blocks = row_data.reshape(modalities.shape[0], BLOCK, row_data.shape[1])

    def one_block(block_pair):
        return select_product(block_pair[0], block_pair[1], text_mat, image_mat, contract)

    result = lax.map(one_block, (blocks, modalities))
    return result.reshape(row_data.shape[0], result.shape[2])


def on_device(tokens, weights, block_modality, doc_ids, grad_out):
    local_rows = tokens.shape[0]
    width_rows = weights.shape[0]
    head_width = weights.shape[3]
    head_count = head_width // HD
    dp_devices = lax.axis_size("dp")
    local_blocks = local_rows // BLOCK
    front_pad = SPAN * local_rows
    window_len = front_pad + local_rows
    my_index = lax.axis_index("dp")
    scale_factor = HD ** (-0.5)
    my_mods = lax.dynamic_slice_in_dim(block_modality, my_index * local_blocks, local_blocks, 0)
    flat_weights = weights.reshape(width_rows, 2, 3 * head_width)
    text_local = flat_weights[:, 0]
    image_local = flat_weights[:, 1]
    columns = lax.all_to_all(tokens, "dp", split_axis=1, concat_axis=0, tiled=True)
    text_whole, image_whole = (
        lax.all_gather(text_local, "dp", axis=0, tiled=True),
        lax.all_gather(image_local, "dp", axis=0, tiled=True),
    )
    summed = blockwise(tokens, my_mods, text_whole, image_whole, 0)
    qkv = summed.astype(jnp.bfloat16).reshape(local_rows, 3, head_count, HD)
    queries = qkv[:, 0]
    key_values = qkv[:, 1:]
    received = []
    for distance in range(SPAN, 0, -1):
        received.append(shifted(key_values, "dp", distance))
    window = jnp.concatenate(received + [key_values], 0)
    key_rows = window[:, 0]
    value_rows = window[:, 1]
    docs_pad = jnp.concatenate([jnp.full((front_pad,), -1, jnp.int32), doc_ids], 0)
    key_docs = lax.dynamic_slice_in_dim(docs_pad, my_index * local_rows, window_len, 0)
    query_docs = lax.dynamic_slice_in_dim(doc_ids, my_index * local_rows, local_rows, 0)
    offsets = jnp.arange(window_len, dtype=jnp.int32) - front_pad
    allowed = (key_docs[None, :] == query_docs[:, None]) & (
        offsets[None, :] <= jnp.arange(local_rows, dtype=jnp.int32)[:, None]
    )
    scores = (
        jnp.einsum("qhd,khd->hqk", queries, key_rows, preferred_element_type=jnp.float32)
        * scale_factor
    )
    scores = jnp.where(allowed[None], scores, -1e30)
    top_score = jnp.max(scores, axis=-1, keepdims=True)
    expos = jnp.where(allowed[None], jnp.exp(scores - top_score), 0.0)
    probs_f = expos / jnp.sum(expos, axis=-1, keepdims=True)
    probs = probs_f.astype(jnp.bfloat16)
    attended = jnp.einsum("hqk,khd->qhd", probs, value_rows, preferred_element_type=jnp.float32)
    attended = attended.astype(jnp.bfloat16).reshape(local_rows, head_width)
    upstream = grad_out.reshape(local_rows, head_count, HD)
    dprob = jnp.einsum("qhd,khd->hqk", upstream, value_rows, preferred_element_type=jnp.float32)
    row_delta = jnp.sum(probs_f * dprob, axis=-1, keepdims=True)
    dscore = (probs_f * (dprob - row_delta)).astype(jnp.bfloat16)
    grad_q = (
        jnp.einsum("hqk,khd->qhd", dscore, key_rows, preferred_element_type=jnp.float32)
        * scale_factor
    )
    grad_k = (
        jnp.einsum("hqk,qhd->khd", dscore, queries, preferred_element_type=jnp.float32)
        * scale_factor
    )
    grad_v = jnp.einsum("hqk,qhd->khd", probs, upstream, preferred_element_type=jnp.float32)
    window_grads = jnp.stack([grad_k, grad_v], 1)
    own_grads = window_grads[front_pad:]
    for distance in range(1, SPAN + 1):
        lower_edge = front_pad - distance * local_rows
        sent_block = window_grads[lower_edge : lower_edge + local_rows]
        own_grads = own_grads + shifted(sent_block.astype(jnp.bfloat16), "dp", -distance).astype(
            sent_block.dtype
        )
    dqkv = (
        jnp.concatenate([grad_q[:, None], own_grads], 1)
        .astype(jnp.bfloat16)
        .reshape(local_rows, 3 * head_width)
    )
    gathered = lax.all_gather(dqkv, "dp", axis=0, tiled=True)
    column_groups = columns.reshape(dp_devices, local_blocks, BLOCK, width_rows)
    grad_groups = gathered.reshape(dp_devices, local_blocks, BLOCK, 3 * head_width)
    modality_groups = block_modality.reshape(dp_devices, local_blocks)
    modality_range = jnp.arange(2, dtype=jnp.int32)

    def accumulate(running, triple):
        column_group, grad_group, group_mods = triple
        per_block = jnp.einsum(
            "bnf,bnc->bfc", column_group, grad_group, preferred_element_type=jnp.float32
        )
        selector = (group_mods[:, None] == modality_range[None, :]).astype(jnp.float32)
        return (running + jnp.sum(selector[:, :, None, None] * per_block[:, None], axis=0), None)

    weight_sum, unused = lax.scan(
        accumulate,
        jnp.zeros((2, width_rows, 3 * head_width), jnp.float32),
        (column_groups, grad_groups, modality_groups),
    )
    grad_weights = (
        jnp.transpose(weight_sum, (1, 0, 2))
        .astype(jnp.bfloat16)
        .reshape(width_rows, 2, 3, head_width)
    )
    input_terms = blockwise(dqkv, my_mods, text_whole, image_whole, 1)
    grad_tokens = lax.psum_scatter(
        input_terms.astype(jnp.bfloat16), "mp", scatter_dimension=1, tiled=True
    )
    return (attended, grad_tokens, grad_weights)


def solution(mesh):
    return jax.shard_map(
        on_device,
        mesh=mesh,
        in_specs=(P("dp", None), P("dp", None, None, "mp"), P(), P(), P("dp", "mp")),
        out_specs=(P("dp", "mp"), P("dp", "mp"), P("dp", None, None, "mp")),
        check_vma=False,
    )
```

profile of v0, /device:TPU:3, one launch (start us, length us, event | category | flops | bytes accessed | tf_op | source)
XLA Modules:
  0.0 913.2 jit_solution(1132027403472162520)
XLA Ops:
  7.2 16.1 %copy.58 = bf16[512,2,3,1024]{0,3,2,1:T(8,128)(2,1)} copy(bf16[512,2,3,1024]{3,1,2,0:T(2,128)(2,1)} %param.16) | data formatting | bytes 12582912 | tf_op args[1]
  23.3 5.9 fusion.37
  30.1 131.2 %all-gather.8.cloned.1.call-done = bf16[4096,1,3072]{0,2,1:T(8,128)(2,1)} async-done(((bf16[512,1,3072]{0,2,1:T(8,128)(2,1)}), bf16[4096,1,3072]{0,2,1:T(8,128)(2,1)}) %all-gather.8.cloned.1.call-update) | async-done | bytes 25165840 | tf_op jit(solution)/shard_map/all_gather | solution.py:58
  161.3 33.1 %copy.59 = bf16[4096,3072]{1,0:T(8,128)(2,1)} copy(bf16[4096,3072]{0,1:T(8,128)(2,1)} %bitcast.130) | data formatting | bytes 50331648 | tf_op jit(solution)/shard_map/while | solution.py:36
  194.4 99.0 %all-gather.10.cloned.1.call-done = bf16[4096,1,3072]{0,2,1:T(8,128)(2,1)} async-done(((bf16[512,1,3072]{0,2,1:T(8,128)(2,1)}), bf16[4096,1,3072]{0,2,1:T(8,128)(2,1)}) %all-gather.10.cloned.1.call-update) | async-done | bytes 25165840 | tf_op jit(solution)/shard_map/all_gather | solution.py:57
  293.4 32.6 %copy.60 = bf16[4096,3072]{1,0:T(8,128)(2,1)} copy(bf16[4096,3072]{0,1:T(8,128)(2,1)} %bitcast.131) | data formatting | bytes 50331648 | tf_op jit(solution)/shard_map/while | solution.py:36
  326.0 28.5 %while.31 = (s32[]{:T(128)}, bf16[2,128,3072]{2,1,0:T(8,128)(2,1)S(1)}, s32[2]{0:T(128)S(1)}, bf16[2,128,4096]{2,1,0:T(8,128)(2,1)}, bf16[4096,3072]{1,0:T(8,128...) while((s32[]{:T(128)}, bf16[2,128,3072]{2,1,0:T(8,128)(2,1)S(1)}, s32[2]{0:T(128)S(1)}, ...), condition=%wide.region_3.4_spmd, body=%wide.region_0.3_spmd.sunk | while | flops 3221225472 | bytes 30671016 | solution.py:36
  328.6 11.6 %conditional.4 = (bf16[1,128,3072]{2,1,0:T(8,128)(2,1)S(1)}) conditional(s32[]{:T(128)} %bitcast.123, (bf16[128,4096]{1,0:T(8,128)(2,1)S(1)}, bf16[4096,3072]{1,0:T(8,128)(2,1)}) %tuple.91, (bf16[128,4096]{1,0:T(8,128)(2,1)S(1)}, bf16[4096,3072]{1,0:T(8,128)(2,1)}) %tuple.92), branch_computations={%region_1.1_spmd, %region_2.2_spmd} | conditional | flops 3221225472 | bytes 27000840 | solution.py:19
  328.6 11.6 %convolution_bitcast_fusion = bf16[1,128,3072]{2,1,0:T(8,128)(2,1)S(1)} fusion(bf16[128,4096]{1,0:T(8,128)(2,1)S(1)} %get-tuple-element.96, bf16[4096,3072]{1,0:T(8,128)(2,1)} %get-tuple-element.97), kind=kOutput, calls=%fused_computation.1 | convolution fusion | flops 3221225472 | bytes 27000832 | tf_op jit(solution)/shard_map/while/body/eval_jaxpr/cond/branch_0_fun/dot_general | solution.py:24
  342.8 11.6 %conditional.4 = (bf16[1,128,3072]{2,1,0:T(8,128)(2,1)S(1)}) conditional(s32[]{:T(128)} %bitcast.123, (bf16[128,4096]{1,0:T(8,128)(2,1)S(1)}, bf16[4096,3072]{1,0:T(8,128)(2,1)}) %tuple.91, (bf16[128,4096]{1,0:T(8,128)(2,1)S(1)}, bf16[4096,3072]{1,0:T(8,128)(2,1)}) %tuple.92), branch_computations={%region_1.1_spmd, %region_2.2_spmd} | conditional | flops 3221225472 | bytes 27000840 | solution.py:19
  342.8 11.6 %convolution_bitcast_fusion.1 = bf16[1,128,3072]{2,1,0:T(8,128)(2,1)S(1)} fusion(bf16[128,4096]{1,0:T(8,128)(2,1)S(1)} %get-tuple-element.98, bf16[4096,3072]{1,0:T(8,128)(2,1)} %get-tuple-element.99), kind=kOutput, calls=%fused_computation.2 | convolution fusion | flops 3221225472 | bytes 27000832 | tf_op jit(solution)/shard_map/while/body/eval_jaxpr/cond/branch_1_fun/dot_general | solution.py:21
  370.5 13.1 %collective-permute-done = bf16[256,2,8,128]{3,0,2,1:T(8,128)(2,1)} collective-permute-done((bf16[256,2,8,128]{3,0,2,1:T(8,128)(2,1)}, bf16[256,2,8,128]{3,0,2,1:T(8,128)(2,1)}, u32[]{:S(2)}, u32[]{:S(2)}) %collective-permute-start) | collective-permute-done | bytes 1048608 | tf_op jit(solution)/shard_map/ppermute | solution.py:14
  386.0 9.5 %collective-permute-done.1 = bf16[256,2,8,128]{3,0,2,1:T(8,128)(2,1)} collective-permute-done((bf16[256,2,8,128]{3,0,2,1:T(8,128)(2,1)}, bf16[256,2,8,128]{3,0,2,1:T(8,128)(2,1)}, u32[]{:S(2)}, u32[]{:S(2)}) %collective-permute-start.1) | collective-permute-done | bytes 1048608 | tf_op jit(solution)/shard_map/ppermute | solution.py:14
  400.4 9.4 %collective-permute-done.3 = bf16[256,2,8,128]{3,0,2,1:T(8,128)(2,1)} collective-permute-done((bf16[256,2,8,128]{3,0,2,1:T(8,128)(2,1)}, bf16[256,2,8,128]{3,0,2,1:T(8,128)(2,1)}, u32[]{:S(2)}, u32[]{:S(2)}) %collective-permute-start.3) | collective-permute-done | bytes 1048608 | tf_op jit(solution)/shard_map/ppermute | solution.py:14
  413.4 10.3 %fusion.39 = (f32[8,256]{1,0:T(8,128)S(1)}, f32[8,256,1280]{2,1,0:T(8,128)}) fusion(pred[256,1280]{1,0:T(8,128)(4,1)S(1)} %fusion.31, bf16[1280,2,8,128]{3,0,2,1:T(8,128)(2,1)} %constant_dynamic-update-slice_fusion.2, bf16[256,1,8,128]{3,2,1,0:T(8,128)(2,1)S(1)} %slice.52), kind=kOutput, calls=%fused_computation.70 | convolution fusion | flops 684197120 | bytes 14295040 | tf_op jit(solution)/shard_map/sub | solution.py:83
  423.7 9.6 %fusion.11 = (f32[8,256]{1,0:T(8,128)S(1)}, f32[8,1280,256]{1,2,0:T(8,128)}) fusion(f32[8,256,1280]{2,1,0:T(8,128)} %get-tuple-element.264, f32[8,256]{1,0:T(8,128)S(1)} %get-tuple-element.263, bf16[256,8,128]{0,2,1:T(8,128)(2,1)S(1)} %bitcast.144, bf16[1280,2,8,128]{3,0,2,1:T(8,128)(2,1)} %constant_dynamic-update-slice_fusion.2), kind=kOutput, calls=%fused_computation.27 | convolution fusion | flops 678950912 | bytes 24133632 | tf_op jit(solution)/shard_map/qhd,khd->hqk/dot_general | solution.py:89
  443.8 5.6 fusion.10
  453.4 29.6 %collective-permute-start.6 = (bf16[256,2,8,128]{0,3,2,1:T(8,128)(2,1)S(1)}, bf16[256,2,8,128]{0,3,2,1:T(8,128)(2,1)S(1)}, u32[]{:S(2)}, u32[]{:S(2)}) collective-permute-start(bf16[256,2,8,128]{0,3,2,1:T(8,128)(2,1)S(1)} %get-tuple-element.261), channel_id=1, source_target_pairs={{12,0},{16,4},{20,8},{24,12},{28,16},{13,1},{17,5},{21,9},{25,13},... | collective-permute-start | bytes 3145736 | tf_op jit(solution)/shard_map/ppermute | solution.py:14
  483.0 9.2 %collective-permute-start.5 = (bf16[256,2,8,128]{0,3,2,1:T(8,128)(2,1)S(1)}, bf16[256,2,8,128]{0,3,2,1:T(8,128)(2,1)S(1)}, u32[]{:S(2)}, u32[]{:S(2)}) collective-permute-start(bf16[256,2,8,128]{0,3,2,1:T(8,128)(2,1)S(1)} %get-tuple-element.262), channel_id=1, source_target_pairs={{8,0},{12,4},{16,8},{20,12},{24,16},{28,20},{9,1},{13,5},{17,9},{2... | collective-permute-start | bytes 3145736 | tf_op jit(solution)/shard_map/ppermute | solution.py:14
  497.9 6.2 collective-permute-done.6
  504.0 30.6 %collective-permute-done.5 = bf16[256,2,8,128]{0,3,2,1:T(8,128)(2,1)S(1)} collective-permute-done((bf16[256,2,8,128]{0,3,2,1:T(8,128)(2,1)S(1)}, bf16[256,2,8,128]{0,3,2,1:T(8,128)(2,1)S(1)}, u32[]{:S(2)}, u32[]{:S(2)}) %collective-permute-start.5) | collective-permute-done | bytes 1048608 | tf_op jit(solution)/shard_map/ppermute | solution.py:14
  548.7 39.6 %all-to-all-done = bf16[256,8,512]{0,2,1:T(8,128)(2,1)S(1)} async-done(((bf16[256,8,512]{0,2,1:T(8,128)(2,1)}), bf16[256,8,512]{0,2,1:T(8,128)(2,1)S(1)}, u32[]{:S(2)}, u32[]{:S(2)}) %all-to-all-start) | async-done | bytes 2097184 | tf_op jit(solution)/shard_map/all_to_all | solution.py:55
  590.6 6.8 fusion.32
  603.9 31.0 %while.32 = (s32[]{:T(128)}, bf16[2,128,4096]{2,1,0:T(8,128)(2,1)}, s32[2]{0:T(128)S(1)}, bf16[2,128,3072]{2,1,0:T(8,128)(2,1)S(1)}, bf16[4096,3072]{1,0:T(8,128...) while((s32[]{:T(128)}, bf16[2,128,4096]{2,1,0:T(8,128)(2,1)}, s32[2]{0:T(128)S(1)}, ...), condition=%wide.region_10.11_spmd, body=%wide.region_7.10_spmd.sunk | while | flops 3221225472 | bytes 30671016 | solution.py:36
  605.3 13.1 %conditional.5 = (bf16[1,128,4096]{2,1,0:T(8,128)(2,1)S(1)}) conditional(s32[]{:T(128)} %bitcast.125, (bf16[128,3072]{1,0:T(8,128)(2,1)S(1)}, bf16[4096,3072]{1,0:T(8,128)(2,1)}) %tuple.94, (bf16[128,3072]{1,0:T(8,128)(2,1)S(1)}, bf16[4096,3072]{1,0:T(8,128)(2,1)}) %tuple.95), branch_computations={%region_8.8_spmd, %region_9.9_spmd} | conditional | flops 3221225472 | bytes 27000840 | solution.py:19
  605.3 13.1 %convolution_bitcast_fusion.2 = bf16[1,128,4096]{2,1,0:T(8,128)(2,1)S(1)} fusion(bf16[128,3072]{1,0:T(8,128)(2,1)S(1)} %get-tuple-element.107, bf16[4096,3072]{1,0:T(8,128)(2,1)} %get-tuple-element.108), kind=kOutput, calls=%fused_computation.5 | convolution fusion | flops 3221225472 | bytes 27000832 | tf_op jit(solution)/shard_map/while/body/eval_jaxpr/cond/branch_0_fun/dot_general | solution.py:24
  620.8 13.1 %conditional.5 = (bf16[1,128,4096]{2,1,0:T(8,128)(2,1)S(1)}) conditional(s32[]{:T(128)} %bitcast.125, (bf16[128,3072]{1,0:T(8,128)(2,1)S(1)}, bf16[4096,3072]{1,0:T(8,128)(2,1)}) %tuple.94, (bf16[128,3072]{1,0:T(8,128)(2,1)S(1)}, bf16[4096,3072]{1,0:T(8,128)(2,1)}) %tuple.95), branch_computations={%region_8.8_spmd, %region_9.9_spmd} | conditional | flops 3221225472 | bytes 27000840 | solution.py:19
  620.8 13.1 %convolution_bitcast_fusion.3 = bf16[1,128,4096]{2,1,0:T(8,128)(2,1)S(1)} fusion(bf16[128,3072]{1,0:T(8,128)(2,1)S(1)} %get-tuple-element.109, bf16[4096,3072]{1,0:T(8,128)(2,1)} %get-tuple-element.110), kind=kOutput, calls=%fused_computation.6 | convolution fusion | flops 3221225472 | bytes 27000832 | tf_op jit(solution)/shard_map/while/body/eval_jaxpr/cond/branch_1_fun/dot_general | solution.py:21
  637.0 16.2 %copy.74 = bf16[2048,3072]{1,0:T(8,128)(2,1)} copy(bf16[2048,3072]{0,1:T(8,128)(2,1)} %all-gather.6.cloned.1.call-done) | data formatting | bytes 25165824 | tf_op jit(solution)/shard_map/all_gather | solution.py:114
  653.2 227.1 %while.33 = (s32[]{:T(128)}, f32[2,512,3072]{2,1,0:T(8,128)}, s32[8,2]{1,0:T(8,128)S(1)}, bf16[8,2,128,512]{3,2,1,0:T(8,128)(2,1)}, bf16[8,2,128,3072]{3,2,1,0:T(8,128)(2,1)}, /*index=5*/s32[]{:T(128)}, s32[]{:T(128)}) while((s32[]{:T(128)}, f32[2,512,3072]{2,1,0:T(8,128)}, s32[8,2]{1,0:T(8,128)S(1)}, ...), condition=%wide.region_14.15_spmd.clone, body=%wide.region_12.14_spmd.clone.sunk | while | flops 821035008 | bytes 77333656 | solution.py:128
  656.6 10.4 %multiply_reduce_fusion.2 = f32[2,512,3072]{2,1,0:T(8,128)} fusion(f32[2,512,3072]{2,1,0:T(8,128)S(1)} %fusion.58, f32[2,2]{1,0:T(2,128)S(1)} %compare_convert_fusion.2), kind=kLoop, calls=%fused_computation.9.clone.1 | loop fusion | flops 9437184 | bytes 25165840 | tf_op jit(solution)/shard_map/while/body/eval_jaxpr/reduce_sum | solution.py:126
  667.0 12.1 %select_add_fusion.2 = f32[2,512,3072]{2,1,0:T(8,128)} fusion(f32[2,512,3072]{2,1,0:T(8,128)} %multiply_reduce_fusion.2, f32[2,512,3072]{2,1,0:T(8,128)} %get-tuple-element.430, pred[]{:T(512)S(6)} %compare.4), kind=kLoop, calls=%fused_computation.10.clone.1 | loop fusion | flops 6291456 | bytes 37748736 | tf_op jit(solution)/shard_map/while/body/eval_jaxpr/add | solution.py:126
  682.6 10.4 %multiply_reduce_fusion.2 = f32[2,512,3072]{2,1,0:T(8,128)} fusion(f32[2,512,3072]{2,1,0:T(8,128)S(1)} %fusion.58, f32[2,2]{1,0:T(2,128)S(1)} %compare_convert_fusion.2), kind=kLoop, calls=%fused_computation.9.clone.1 | loop fusion | flops 9437184 | bytes 25165840 | tf_op jit(solution)/shard_map/while/body/eval_jaxpr/reduce_sum | solution.py:126
  693.0 14.9 %select_add_fusion.2 = f32[2,512,3072]{2,1,0:T(8,128)} fusion(f32[2,512,3072]{2,1,0:T(8,128)} %multiply_reduce_fusion.2, f32[2,512,3072]{2,1,0:T(8,128)} %get-tuple-element.430, pred[]{:T(512)S(6)} %compare.4), kind=kLoop, calls=%fused_computation.10.clone.1 | loop fusion | flops 6291456 | bytes 37748736 | tf_op jit(solution)/shard_map/while/body/eval_jaxpr/add | solution.py:126
  711.3 10.4 %multiply_reduce_fusion.2 = f32[2,512,3072]{2,1,0:T(8,128)} fusion(f32[2,512,3072]{2,1,0:T(8,128)S(1)} %fusion.58, f32[2,2]{1,0:T(2,128)S(1)} %compare_convert_fusion.2), kind=kLoop, calls=%fused_computation.9.clone.1 | loop fusion | flops 9437184 | bytes 25165840 | tf_op jit(solution)/shard_map/while/body/eval_jaxpr/reduce_sum | solution.py:126
  721.7 14.9 %select_add_fusion.2 = f32[2,512,3072]{2,1,0:T(8,128)} fusion(f32[2,512,3072]{2,1,0:T(8,128)} %multiply_reduce_fusion.2, f32[2,512,3072]{2,1,0:T(8,128)} %get-tuple-element.430, pred[]{:T(512)S(6)} %compare.4), kind=kLoop, calls=%fused_computation.10.clone.1 | loop fusion | flops 6291456 | bytes 37748736 | tf_op jit(solution)/shard_map/while/body/eval_jaxpr/add | solution.py:126
  740.1 10.4 %multiply_reduce_fusion.2 = f32[2,512,3072]{2,1,0:T(8,128)} fusion(f32[2,512,3072]{2,1,0:T(8,128)S(1)} %fusion.58, f32[2,2]{1,0:T(2,128)S(1)} %compare_convert_fusion.2), kind=kLoop, calls=%fused_computation.9.clone.1 | loop fusion | flops 9437184 | bytes 25165840 | tf_op jit(solution)/shard_map/while/body/eval_jaxpr/reduce_sum | solution.py:126
  750.4 14.9 %select_add_fusion.2 = f32[2,512,3072]{2,1,0:T(8,128)} fusion(f32[2,512,3072]{2,1,0:T(8,128)} %multiply_reduce_fusion.2, f32[2,512,3072]{2,1,0:T(8,128)} %get-tuple-element.430, pred[]{:T(512)S(6)} %compare.4), kind=kLoop, calls=%fused_computation.10.clone.1 | loop fusion | flops 6291456 | bytes 37748736 | tf_op jit(solution)/shard_map/while/body/eval_jaxpr/add | solution.py:126
  768.8 10.4 %multiply_reduce_fusion.2 = f32[2,512,3072]{2,1,0:T(8,128)} fusion(f32[2,512,3072]{2,1,0:T(8,128)S(1)} %fusion.58, f32[2,2]{1,0:T(2,128)S(1)} %compare_convert_fusion.2), kind=kLoop, calls=%fused_computation.9.clone.1 | loop fusion | flops 9437184 | bytes 25165840 | tf_op jit(solution)/shard_map/while/body/eval_jaxpr/reduce_sum | solution.py:126
  779.2 14.9 %select_add_fusion.2 = f32[2,512,3072]{2,1,0:T(8,128)} fusion(f32[2,512,3072]{2,1,0:T(8,128)} %multiply_reduce_fusion.2, f32[2,512,3072]{2,1,0:T(8,128)} %get-tuple-element.430, pred[]{:T(512)S(6)} %compare.4), kind=kLoop, calls=%fused_computation.10.clone.1 | loop fusion | flops 6291456 | bytes 37748736 | tf_op jit(solution)/shard_map/while/body/eval_jaxpr/add | solution.py:126
  797.5 10.4 %multiply_reduce_fusion.2 = f32[2,512,3072]{2,1,0:T(8,128)} fusion(f32[2,512,3072]{2,1,0:T(8,128)S(1)} %fusion.58, f32[2,2]{1,0:T(2,128)S(1)} %compare_convert_fusion.2), kind=kLoop, calls=%fused_computation.9.clone.1 | loop fusion | flops 9437184 | bytes 25165840 | tf_op jit(solution)/shard_map/while/body/eval_jaxpr/reduce_sum | solution.py:126
  807.9 14.9 %select_add_fusion.2 = f32[2,512,3072]{2,1,0:T(8,128)} fusion(f32[2,512,3072]{2,1,0:T(8,128)} %multiply_reduce_fusion.2, f32[2,512,3072]{2,1,0:T(8,128)} %get-tuple-element.430, pred[]{:T(512)S(6)} %compare.4), kind=kLoop, calls=%fused_computation.10.clone.1 | loop fusion | flops 6291456 | bytes 37748736 | tf_op jit(solution)/shard_map/while/body/eval_jaxpr/add | solution.py:126
  826.3 10.4 %multiply_reduce_fusion.2 = f32[2,512,3072]{2,1,0:T(8,128)} fusion(f32[2,512,3072]{2,1,0:T(8,128)S(1)} %fusion.58, f32[2,2]{1,0:T(2,128)S(1)} %compare_convert_fusion.2), kind=kLoop, calls=%fused_computation.9.clone.1 | loop fusion | flops 9437184 | bytes 25165840 | tf_op jit(solution)/shard_map/while/body/eval_jaxpr/reduce_sum | solution.py:126
  836.6 14.9 %select_add_fusion.2 = f32[2,512,3072]{2,1,0:T(8,128)} fusion(f32[2,512,3072]{2,1,0:T(8,128)} %multiply_reduce_fusion.2, f32[2,512,3072]{2,1,0:T(8,128)} %get-tuple-element.430, pred[]{:T(512)S(6)} %compare.4), kind=kLoop, calls=%fused_computation.10.clone.1 | loop fusion | flops 6291456 | bytes 37748736 | tf_op jit(solution)/shard_map/while/body/eval_jaxpr/add | solution.py:126
  855.0 10.4 %multiply_reduce_fusion.2 = f32[2,512,3072]{2,1,0:T(8,128)} fusion(f32[2,512,3072]{2,1,0:T(8,128)S(1)} %fusion.58, f32[2,2]{1,0:T(2,128)S(1)} %compare_convert_fusion.2), kind=kLoop, calls=%fused_computation.9.clone.1 | loop fusion | flops 9437184 | bytes 25165840 | tf_op jit(solution)/shard_map/while/body/eval_jaxpr/reduce_sum | solution.py:126
  865.4 14.9 %select_add_fusion.2 = f32[2,512,3072]{2,1,0:T(8,128)} fusion(f32[2,512,3072]{2,1,0:T(8,128)} %multiply_reduce_fusion.2, f32[2,512,3072]{2,1,0:T(8,128)} %get-tuple-element.430, pred[]{:T(512)S(6)} %compare.4), kind=kLoop, calls=%fused_computation.10.clone.1 | loop fusion | flops 6291456 | bytes 37748736 | tf_op jit(solution)/shard_map/while/body/eval_jaxpr/add | solution.py:126
  880.3 10.0 %copy.76 = bf16[2,512,3072]{1,2,0:T(8,128)(2,1)} copy(f32[2,512,3072]{2,1,0:T(8,128)} %get-tuple-element.133) | data formatting | bytes 18874368 | tf_op jit(solution)/shard_map/while | solution.py:128
  890.3 16.3 %copy.78 = bf16[512,2,3,1024]{3,1,2,0:T(2,128)(2,1)} copy(bf16[512,2,3,1024]{0,3,2,1:T(8,128)(2,1)} %bitcast.133) | data formatting | bytes 12582912
  (107 shorter events, 107.3 us)
Async XLA Ops:
  7.2 154.1 %all-gather.8.cloned.1.call-start = ((), (), s32[]{:S(2)}) async-start(), calls=%async_computation.4 | async-start | bytes 28311552 | tf_op jit(solution)/shard_map/all_gather | solution.py:58
  29.1 0.8 copy-start.6
  29.2 264.3 %all-gather.10.cloned.1.call-start = ((), (), s32[]{:S(2)}) async-start(), calls=%async_computation.5 | async-start | bytes 28311552 | tf_op jit(solution)/shard_map/all_gather | solution.py:57
  29.9 607.1 %all-gather.6.cloned.1.call-start = ((), (), s32[]{:S(2)}) async-start(), calls=%async_computation.3 | async-start | bytes 14155776 | tf_op jit(solution)/shard_map/all_gather | solution.py:114
  354.5 1.1 copy-start.3
  354.5 15.5 %copy-start.5 = (s32[2048]{0:T(1024)S(1)}, s32[2048]{0:T(1024)}, u32[]{:S(2)}) copy-start(s32[2048]{0:T(1024)} %param.18) | copy-start | bytes 24580
  358.8 24.8 %collective-permute-start = (bf16[256,2,8,128]{3,0,2,1:T(8,128)(2,1)}, bf16[256,2,8,128]{3,0,2,1:T(8,128)(2,1)}, u32[]{:S(2)}, u32[]{:S(2)}) collective-permute-start(bf16[256,2,8,128]{3,0,2,1:T(8,128)(2,1)} %copy.84), channel_id=1, source_target_pairs={{0,16},{4,20},{8,24},{12,28},{1,17},{5,21},{9,25},{13,29},{2,18},{... | collective-permute-start | bytes 3145736 | tf_op jit(solution)/shard_map/ppermute | solution.py:14
  362.0 33.5 %collective-permute-start.1 = (bf16[256,2,8,128]{3,0,2,1:T(8,128)(2,1)}, bf16[256,2,8,128]{3,0,2,1:T(8,128)(2,1)}, u32[]{:S(2)}, u32[]{:S(2)}) collective-permute-start(bf16[256,2,8,128]{3,0,2,1:T(8,128)(2,1)} %copy.84), channel_id=1, source_target_pairs={{0,12},{4,16},{8,20},{12,24},{16,28},{1,13},{5,17},{9,21},{13,25},... | collective-permute-start | bytes 3145736 | tf_op jit(solution)/shard_map/ppermute | solution.py:14
  363.9 34.1 %collective-permute-start.2 = (bf16[256,2,8,128]{3,0,2,1:T(8,128)(2,1)}, bf16[256,2,8,128]{3,0,2,1:T(8,128)(2,1)}, u32[]{:S(2)}, u32[]{:S(2)}) collective-permute-start(bf16[256,2,8,128]{3,0,2,1:T(8,128)(2,1)} %copy.84), channel_id=1, source_target_pairs={{0,8},{4,12},{8,16},{12,20},{16,24},{20,28},{1,9},{5,13},{9,17},{1... | collective-permute-start | bytes 3145736 | tf_op jit(solution)/shard_map/ppermute | solution.py:14
  365.8 43.9 %collective-permute-start.3 = (bf16[256,2,8,128]{3,0,2,1:T(8,128)(2,1)}, bf16[256,2,8,128]{3,0,2,1:T(8,128)(2,1)}, u32[]{:S(2)}, u32[]{:S(2)}) collective-permute-start(bf16[256,2,8,128]{3,0,2,1:T(8,128)(2,1)} %copy.84), channel_id=1, source_target_pairs={{0,4},{4,8},{8,12},{12,16},{16,20},{20,24},{24,28},{1,5},{5,9},{9,... | collective-permute-start | bytes 3145736 | tf_op jit(solution)/shard_map/ppermute | solution.py:14
  413.4 10.3 %copy-start.4 = (bf16[256,1024]{0,1:T(8,128)(2,1)S(1)}, bf16[256,1024]{0,1:T(8,128)(2,1)}, u32[]{:S(2)}) copy-start(bf16[256,1024]{0,1:T(8,128)(2,1)} %copy.86) | copy-start | bytes 1572868
  423.7 11.4 %copy-start.1 = (f32[8,256,1280]{2,1,0:T(8,128)S(1)}, f32[8,256,1280]{2,1,0:T(8,128)}, u32[]{:S(2)}) copy-start(f32[8,256,1280]{2,1,0:T(8,128)} %get-tuple-element.264) | copy-start | bytes 31457284
  435.1 5.9 copy-start.2
  449.4 88.6 %slice-start = ((s8[5242880]{0:T(1024)(128)(4,1)}), s8[4194304]{0:T(1024)(128)(4,1)S(1)}, s32[]{:S(2)}) async-start(s8[5242880]{0:T(1024)(128)(4,1)} %bitcast.134), calls=%async_computation.6 | async-start | bytes 8388608
  452.1 45.8 %collective-permute-start.7 = (bf16[256,2,8,128]{0,3,2,1:T(8,128)(2,1)S(1)}, bf16[256,2,8,128]{0,3,2,1:T(8,128)(2,1)S(1)}, u32[]{:S(2)}, u32[]{:S(2)}) collective-permute-start(bf16[256,2,8,128]{0,3,2,1:T(8,128)(2,1)S(1)} %get-tuple-element.260), channel_id=1, source_target_pairs={{16,0},{20,4},{24,8},{28,12},{17,1},{21,5},{25,9},{29,13},{18,2},{... | collective-permute-start | bytes 3145736 | tf_op jit(solution)/shard_map/ppermute | solution.py:14
  453.4 50.7 %collective-permute-start.6 = (bf16[256,2,8,128]{0,3,2,1:T(8,128)(2,1)S(1)}, bf16[256,2,8,128]{0,3,2,1:T(8,128)(2,1)S(1)}, u32[]{:S(2)}, u32[]{:S(2)}) collective-permute-start(bf16[256,2,8,128]{0,3,2,1:T(8,128)(2,1)S(1)} %get-tuple-element.261), channel_id=1, source_target_pairs={{12,0},{16,4},{20,8},{24,12},{28,16},{13,1},{17,5},{21,9},{25,13},... | collective-permute-start | bytes 3145736 | tf_op jit(solution)/shard_map/ppermute | solution.py:14
  483.0 51.7 %collective-permute-start.5 = (bf16[256,2,8,128]{0,3,2,1:T(8,128)(2,1)S(1)}, bf16[256,2,8,128]{0,3,2,1:T(8,128)(2,1)S(1)}, u32[]{:S(2)}, u32[]{:S(2)}) collective-permute-start(bf16[256,2,8,128]{0,3,2,1:T(8,128)(2,1)S(1)} %get-tuple-element.262), channel_id=1, source_target_pairs={{8,0},{12,4},{16,8},{20,12},{24,16},{28,20},{9,1},{13,5},{17,9},{2... | collective-permute-start | bytes 3145736 | tf_op jit(solution)/shard_map/ppermute | solution.py:14
  492.2 45.8 %slice-start.1 = ((s8[5242880]{0:T(1024)(128)(4,1)}), s8[1048576]{0:T(1024)(128)(4,1)S(1)}, s32[]{:S(2)}) async-start(s8[5242880]{0:T(1024)(128)(4,1)} %bitcast.134), calls=%async_computation.7 | async-start | bytes 2097152
  492.2 45.8 %collective-permute-start.4 = (bf16[256,2,8,128]{0,3,2,1:T(8,128)(2,1)S(1)}, bf16[256,2,8,128]{0,3,2,1:T(8,128)(2,1)S(1)}, u32[]{:S(2)}, u32[]{:S(2)}) collective-permute-start(bf16[256,2,8,128]{0,3,2,1:T(8,128)(2,1)S(1)} %get-tuple-element.259), channel_id=1, source_target_pairs={{4,0},{8,4},{12,8},{16,12},{20,16},{24,20},{28,24},{5,1},{9,5},{13... | collective-permute-start | bytes 3145736 | tf_op jit(solution)/shard_map/ppermute | solution.py:14
  540.1 8.5 copy-start.7
  544.2 44.0 %all-to-all-start = ((bf16[256,8,512]{0,2,1:T(8,128)(2,1)}), bf16[256,8,512]{0,2,1:T(8,128)(2,1)S(1)}, u32[]{:S(2)}, u32[]{:S(2)}) async-start(bf16[256,8,512]{0,2,1:T(8,128)(2,1)} %bitcast.138), calls=%async_computation.1 | async-start | bytes 4194304 | tf_op jit(solution)/shard_map/all_to_all | solution.py:55
  548.6 358.0 %reduce-scatter.2.cloned.1.call-start = ((), (), s32[]{:S(2)}) async-start(), calls=%async_computation.2 | async-start | bytes 2621440 | tf_op jit(solution)/shard_map/reduce_scatter | solution.py:139
  590.6 7.8 copy-start
Sparse Core Ops, SparseCore 0:
  29.3 131.9 all-gather.7
  163.1 130.2 all-gather.9
  540.3 96.6 all-gather.5
  639.7 43.2 reduce-scatter.1
where the time goes:
time: 922 us; the launch traced here: 913 us
  waiting for transfers between devices  345 us (37%)
  other arithmetic  210 us (23%)
  local copies, waits for them, and re-layouts  175 us (19%)
  matrix products  111 us (12%)
  starting transfers between devices  55.7 us (6%)
  between operations  14 us (2%)
    all_gather x1, waiting for transfers between devices, on_device(): lax.all_gather(image_local, 'dp', axis=0, tiled=True)  131 us
    add x8, other arithmetic, accumulate(): running + jnp.sum(selector[:, :, None, None] * per_block[:, None], axis=0)  117 us
    all_gather x1, waiting for transfers between devices, on_device(): lax.all_gather(text_local, 'dp', axis=0, tiled=True)  99 us
    reduce_sum x8, other arithmetic, accumulate(): jnp.sum(selector[:, :, None, None] * per_block[:, None], axis=0)  83 us
    ppermute x8, waiting for transfers between devices, shifted(): return lax.ppermute(block, axis, route)  72.1 us
    while x3, local copies, waits for them, and re-layouts, blockwise(): result = lax.map(one_block, (blocks, modalities))  69.4 us
    unnamed x30, local copies, waits for them, and re-layouts  55.6 us
    ppermute x8, starting transfers between devices, shifted(): return lax.ppermute(block, axis, route)  51.2 us
  transfers between devices with their start and end apart: 13, of which 10 were waited for; matrix products, arithmetic and copies ran while one was open for 40% of the time, Pallas kernels for 0%

commit v1 on v0

--- a/solution.py
+++ b/solution.py
@@ -1,6 +1,10 @@
+import functools
+
 import jax
 import jax.numpy as jnp
 from jax import lax
+from jax.experimental import pallas as pl
+from jax.experimental.pallas import tpu as pltpu
 from jax.sharding import PartitionSpec as P
 
 HD = 128
@@ -37,7 +41,7 @@
     return result.reshape(row_data.shape[0], result.shape[2])
 
 
-def on_device(tokens, weights, block_modality, doc_ids, grad_out):
+def windowed(tokens, weights, block_modality, doc_ids, grad_out):
     local_rows = tokens.shape[0]
     width_rows = weights.shape[0]
     head_width = weights.shape[3]
@@ -142,6 +146,258 @@
     return (attended, grad_tokens, grad_weights)
 
 
+VMEM_LIMIT = 56 * 1024 * 1024
+NT = (((1,), (1,)), ((), ()))
+TN = (((0,), (0,)), ((), ()))
+
+
+def dot_f32(a, b, dims=(((1,), (0,)), ((), ()))):
+    return lax.dot_general(a, b, dims, preferred_element_type=jnp.float32)
+
+
+def params():
+    return pltpu.CompilerParams(vmem_limit_bytes=VMEM_LIMIT)
+
+
+def project_kernel(pair, mods_ref, x_ref, w_ref, out_ref):
+    blocks = x_ref.shape[0] // BLOCK
+
+    def one(b, carry):
+        rows = pl.ds(pl.multiple_of(b * BLOCK, BLOCK), BLOCK)
+        x = x_ref[rows, :]
+        modality = mods_ref[b]
+        for p in range(3):
+            y = dot_f32(x, w_ref[modality, p]).astype(jnp.bfloat16)
+            for h in range(pair):
+                out_ref[h, rows, p * HD : (p + 1) * HD] = y[:, h * HD : (h + 1) * HD]
+        return carry
+
+    lax.fori_loop(0, blocks, one, 0, unroll=4)
+
+
+def project(columns, planes, block_modality, pair):
+    rows, width = columns.shape
+    heads = planes.shape[3] // HD
+    return pl.pallas_call(
+        functools.partial(project_kernel, pair),
+        out_shape=jax.ShapeDtypeStruct((heads, rows, 3 * HD), jnp.bfloat16),
+        grid_spec=pltpu.PrefetchScalarGridSpec(
+            num_scalar_prefetch=1,
+            grid=(heads // pair,),
+            in_specs=[
+                pl.BlockSpec((rows, width), lambda h, m: (0, 0)),
+                pl.BlockSpec((2, 3, width, pair * HD), lambda h, m: (0, 0, 0, h)),
+            ],
+            out_specs=pl.BlockSpec((pair, rows, 3 * HD), lambda h, m: (h, 0, 0)),
+        ),
+        compiler_params=params(),
+        name="project",
+    )(block_modality, columns, planes)
+
+
+def attention_kernel(step, window, qkv_ref, g_ref, col_ref, row_ref, att_ref, grad_ref, dk_acc, dv_acc):
+    i = pl.program_id(1)
+    scale = HD ** (-0.5)
+    low = pl.multiple_of(jnp.maximum((i + 1) * step - window, 0), step)
+    mine = pl.ds(pl.multiple_of(i * step, step), step)
+    seen = pl.ds(low, window)
+
+    @pl.when(i == 0)
+    def _():
+        dk_acc[...] = jnp.zeros_like(dk_acc)
+        dv_acc[...] = jnp.zeros_like(dv_acc)
+
+    q = qkv_ref[0, mine, 0:HD]
+    k = qkv_ref[0, seen, HD : 2 * HD]
+    v = qkv_ref[0, seen, 2 * HD : 3 * HD]
+    g = g_ref[0, mine, :]
+    gap = (i * step - low).astype(jnp.int32)
+    ahead = lax.broadcasted_iota(jnp.int32, (step, window), 1) - lax.broadcasted_iota(
+        jnp.int32, (step, window), 0
+    )
+    allowed = (col_ref[mine, :] == row_ref[:, seen]) & (ahead <= gap)
+    scores = jnp.where(allowed, dot_f32(q, k, NT) * scale, -1e30)
+    top = jnp.max(scores, axis=1, keepdims=True)
+    expos = jnp.where(allowed, jnp.exp(scores - top), 0.0)
+    probs_f = expos * (1.0 / jnp.sum(expos, axis=1, keepdims=True))
+    probs = probs_f.astype(jnp.bfloat16)
+    att_ref[0, mine, :] = dot_f32(probs, v).astype(jnp.bfloat16)
+    dprob = dot_f32(g, v, NT)
+    delta = jnp.sum(probs_f * dprob, axis=1, keepdims=True)
+    dscore = (probs_f * (dprob - delta)).astype(jnp.bfloat16)
+    grad_ref[0, mine, 0:HD] = (dot_f32(dscore, k) * scale).astype(jnp.bfloat16)
+    dk_acc[seen, :] += dot_f32(dscore, q, TN)
+    dv_acc[seen, :] += dot_f32(probs, g, TN)
+
+    @pl.when(i == pl.num_programs(1) - 1)
+    def _():
+        grad_ref[0, :, HD : 2 * HD] = (dk_acc[...] * scale).astype(jnp.bfloat16)
+        grad_ref[0, :, 2 * HD : 3 * HD] = dv_acc[...].astype(jnp.bfloat16)
+
+
+def attention(qkv, upstream, doc_ids, step):
+    heads, rows, width = qkv.shape
+    window = min((SPAN + 1) * step, rows)
+    whole = lambda h, i: (h, 0, 0)
+    fixed = lambda h, i: (0, 0)
+    return pl.pallas_call(
+        functools.partial(attention_kernel, step, window),
+        out_shape=(
+            jax.ShapeDtypeStruct((heads, rows, HD), jnp.bfloat16),
+            jax.ShapeDtypeStruct((heads, rows, width), jnp.bfloat16),
+        ),
+        grid=(heads, rows // step),
+        in_specs=[
+            pl.BlockSpec((1, rows, width), whole),
+            pl.BlockSpec((1, rows, HD), whole),
+            pl.BlockSpec((rows, 1), fixed),
+            pl.BlockSpec((1, rows), fixed),
+        ],
+        out_specs=[
+            pl.BlockSpec((1, rows, HD), whole),
+            pl.BlockSpec((1, rows, width), whole),
+        ],
+        scratch_shapes=[pltpu.VMEM((rows, HD), jnp.float32)] * 2,
+        compiler_params=params(),
+        name="attention",
+    )(qkv, upstream, doc_ids[:, None], doc_ids[None, :])
+
+
+def input_kernel(pair, mods_ref, d_ref, w_ref, out_ref, acc):
+    step = pl.program_id(0)
+    blocks = d_ref.shape[1] // BLOCK
+
+    @pl.when(step == 0)
+    def _():
+        acc[...] = jnp.zeros_like(acc)
+
+    def one(b, carry):
+        rows = pl.ds(pl.multiple_of(b * BLOCK, BLOCK), BLOCK)
+        modality = mods_ref[b]
+        total = acc[rows, :]
+        for p in range(3):
+            lhs = jnp.concatenate(
+                [d_ref[h, rows, p * HD : (p + 1) * HD] for h in range(pair)], axis=1
+            )
+            total = total + dot_f32(lhs, w_ref[modality, p], NT)
+        acc[rows, :] = total
+        return carry
+
+    lax.fori_loop(0, blocks, one, 0, unroll=4)
+
+    @pl.when(step == pl.num_programs(0) - 1)
+    def _():
+        out_ref[...] = acc[...].astype(jnp.bfloat16)
+
+
+def input_parts(grads, planes, block_modality, pair):
+    heads, rows, width3 = grads.shape
+    width = planes.shape[2]
+    return pl.pallas_call(
+        functools.partial(input_kernel, pair),
+        out_shape=jax.ShapeDtypeStruct((rows, width), jnp.bfloat16),
+        grid_spec=pltpu.PrefetchScalarGridSpec(
+            num_scalar_prefetch=1,
+            grid=(heads // pair,),
+            in_specs=[
+                pl.BlockSpec((pair, rows, width3), lambda h, m: (h, 0, 0)),
+                pl.BlockSpec((2, 3, width, pair * HD), lambda h, m: (0, 0, 0, h)),
+            ],
+            out_specs=pl.BlockSpec((rows, width), lambda h, m: (0, 0)),
+            scratch_shapes=[pltpu.VMEM((rows, width), jnp.float32)],
+        ),
+        compiler_params=params(),
+        name="input_parts",
+    )(block_modality, grads, planes)
+
+
+def weight_kernel(pair, d_ref, x_ref, out_ref):
+    for p in range(3):
+        rhs = jnp.concatenate([d_ref[h, :, p * HD : (p + 1) * HD] for h in range(pair)], axis=1)
+        for modality in range(2):
+            out_ref[modality, p] = dot_f32(x_ref[modality], rhs).astype(jnp.bfloat16)
+
+
+def weight_grads(grads, flipped, pair):
+    heads, rows, width3 = grads.shape
+    width = flipped.shape[1]
+    return pl.pallas_call(
+        functools.partial(weight_kernel, pair),
+        out_shape=jax.ShapeDtypeStruct((2, 3, width, heads * HD), jnp.bfloat16),
+        grid=(heads // pair,),
+        in_specs=[
+            pl.BlockSpec((pair, rows, width3), lambda h: (h, 0, 0)),
+            pl.BlockSpec((2, width, rows), lambda h: (0, 0, 0)),
+        ],
+        out_specs=pl.BlockSpec((2, 3, width, pair * HD), lambda h: (0, 0, 0, h)),
+        compiler_params=params(),
+        name="weight_grads",
+    )(grads, flipped)
+
+
+def place_inputs(parts):
+    dp, mp = lax.axis_size("dp"), lax.axis_size("mp")
+    ratio = dp // mp
+    summed = lax.psum_scatter(parts, "mp", scatter_dimension=0, tiled=True)
+    rows, width = summed.shape[0] // ratio, summed.shape[1]
+    mine = lax.axis_index("dp")
+    placed = jnp.zeros((rows, ratio * width), summed.dtype)
+    for s in range(ratio):
+        route = [
+            (j * mp + g, (ratio * g + (j + s) % ratio) * mp + j // ratio)
+            for j in range(dp)
+            for g in range(mp)
+        ]
+        sent = lax.dynamic_slice_in_dim(summed, ((mine + s) % ratio) * rows, rows, 0)
+        piece = lax.ppermute(sent, ("dp", "mp"), route)
+        spot = (mine - s + ratio) % ratio
+        placed = lax.dynamic_update_slice_in_dim(placed, piece, spot * width, 1)
+    return placed
+
+
+def by_heads(tokens, weights, block_modality, doc_ids, grad_out):
+    local_rows = tokens.shape[0]
+    head_width = weights.shape[3]
+    heads = head_width // HD
+    dp = lax.axis_size("dp")
+    own = heads // dp
+    total_rows = doc_ids.shape[0]
+    pair = 2 if heads % 2 == 0 else 1
+    columns = lax.all_to_all(tokens, "dp", split_axis=1, concat_axis=0, tiled=True)
+    upstream = lax.all_to_all(
+        grad_out.reshape(local_rows, heads, HD).transpose(1, 0, 2),
+        "dp",
+        split_axis=0,
+        concat_axis=1,
+        tiled=True,
+    )
+    planes = jnp.transpose(weights, (1, 2, 0, 3))
+    partial = project(columns, planes, block_modality, pair)
+    qkv = lax.psum_scatter(partial, "dp", scatter_dimension=0, tiled=True)
+    attended, grads = attention(qkv, upstream, doc_ids, local_rows)
+    attended = attended.reshape(own, dp, local_rows, HD).transpose(1, 0, 2, 3)
+    attended = lax.all_to_all(attended, "dp", split_axis=0, concat_axis=0, tiled=True)
+    attended = attended.reshape(heads, local_rows, HD)
+    attended = attended.transpose(1, 0, 2).reshape(local_rows, head_width)
+    gathered = lax.all_gather(grads, "dp", axis=0, tiled=True)
+    token_mods = jnp.broadcast_to(block_modality[:, None], (total_rows // BLOCK, BLOCK))
+    token_mods = token_mods.reshape(total_rows)
+    mask = token_mods[None, :] == jnp.arange(2, dtype=jnp.int32)[:, None]
+    flipped = jnp.where(mask[:, None, :], columns.T[None], jnp.zeros((), jnp.bfloat16))
+    parts = input_parts(gathered, planes, block_modality, pair)
+    grad_tokens = place_inputs(parts)
+    grad_weights = jnp.transpose(weight_grads(gathered, flipped, pair), (2, 0, 1, 3))
+    return attended, grad_tokens, grad_weights
+
+
+def on_device(tokens, weights, block_modality, doc_ids, grad_out):
+    dp, mp = lax.axis_size("dp"), lax.axis_size("mp")
+    heads = weights.shape[3] // HD
+    if heads % dp == 0 and dp % mp == 0:
+        return by_heads(tokens, weights, block_modality, doc_ids, grad_out)
+    return windowed(tokens, weights, block_modality, doc_ids, grad_out)
+
+
 def solution(mesh):
     return jax.shard_map(
         on_device,

time: 922 us -> 362 us (0.39)
  other arithmetic: 210 us -> 3.9 us
  local copies, waits for them, and re-layouts: 175 us -> 32.8 us
  waiting for transfers between devices: 345 us -> 213 us
  matrix products: 111 us -> 0 us
  Pallas kernels: 0 us -> 76.2 us
  starting transfers between devices: 55.7 us -> 19 us
    all_gather x3 -> x1, waiting for transfers between devices: 232 us -> 72.8 us  [by_heads(): gathered = lax.all_gather(grads, 'dp', axis=0, tiled=True)]
    add x9 -> x0, other arithmetic: 118 us -> none  [the longest x8 117 us: accumulate(): running + jnp.sum(selector[:, :, None, None] * per_block[:, None], axis=0)]
    reduce_scatter x1 -> x2, waiting for transfers between devices: 0.01 us -> 115 us  [the longest x1 78.4 us: by_heads(): qkv = lax.psum_scatter(partial, 'dp', scatter_dimension=0, tiled=True)]
    dot_general x17 -> x0, matrix products: 100 us -> none  [the longest x8 26.7 us: accumulate(): jnp.einsum('bnf,bnc->bfc', column_group, grad_group, preferred_element_ty...]
    reduce_sum x8 -> x0, other arithmetic: 83 us -> none  [accumulate(): jnp.sum(selector[:, :, None, None] * per_block[:, None], axis=0)]
    while x4 -> x0, local copies, waits for them, and re-layouts: 79.4 us -> none  [the longest x3 69.4 us: blockwise(): result = lax.map(one_block, (blocks, modalities))]
    pallas_call x0 -> x4, Pallas kernels: none -> 76.2 us  [the longest x1 23.3 us: input_parts(): pl.pallas_call(functools.partial(input_kernel, pair), out_shape=jax.Shape...]
    ppermute x8 -> x2, waiting for transfers between devices: 72.1 us -> 0.01 us  [place_inputs(): piece = lax.ppermute(sent, ('dp', 'mp'), route)]
  transfers between devices with their start and end apart: 13 -> 8, of which waited for: 10 -> 5; matrix products, arithmetic and copies ran while one was open for 40% -> 9% of each run, Pallas kernels for 0% -> 5%
where the time goes in v1:
time: 362 us; the launch traced here: 358 us
  waiting for transfers between devices  213 us (59%)
  Pallas kernels  76.2 us (21%)
  local copies, waits for them, and re-layouts  32.8 us (9%)
  starting transfers between devices  19 us (5%)
  between operations  13.9 us (4%)
  other arithmetic  3.9 us (1%)
    reduce_scatter x1, waiting for transfers between devices, by_heads(): qkv = lax.psum_scatter(partial, 'dp', scatter_dimension=0, tiled=True)  78.4 us
    all_gather x1, waiting for transfers between devices, by_heads(): gathered = lax.all_gather(grads, 'dp', axis=0, tiled=True)  72.8 us
    reduce_scatter x1, waiting for transfers between devices, place_inputs(): summed = lax.psum_scatter(parts, 'mp', scatter_dimension=0, tiled=True)  36.9 us
    unnamed x19, local copies, waits for them, and re-layouts  23.4 us
    pallas_call x1, Pallas kernels, input_parts(): pl.pallas_call(functools.partial(input_kernel, pair), out_shape=jax.Shape...  23.3 us
    pallas_call x1, Pallas kernels, attention(): pl.pallas_call(functools.partial(attention_kernel, step, window), out_sha...  20.7 us
    pallas_call x1, Pallas kernels, weight_grads(): pl.pallas_call(functools.partial(weight_kernel, pair), out_shape=jax.Shap...  18.1 us
    all_to_all x1, waiting for transfers between devices, by_heads(): lax.all_to_all(tokens, 'dp', split_axis=1, concat_axis=0, tiled=True)  17.5 us
  transfers between devices with their start and end apart: 8, of which 5 were waited for; matrix products, arithmetic and copies ran while one was open for 9% of the time, Pallas kernels for 5%

profile of v1, /device:TPU:3, one launch (start us, length us, event | category | flops | bytes accessed | tf_op | source)
XLA Modules:
  0.0 358.3 jit_solution(8600619890493388719)
XLA Ops:
  7.2 0.0 copy-start
  7.2 3.2 copy.43
  10.4 4.6 %all-to-all-start = ((bf16[256,8,512]{2,0,1:T(8,128)(2,1)}), bf16[256,8,512]{2,0,1:T(8,128)(2,1)S(1)}, u32[]{:S(2)}, u32[]{:S(2)}) async-start(bf16[256,8,512]{2,0,1:T(8,128)(2,1)} %bitcast.38), calls=%async_computation | async-start | bytes 4194304 | tf_op jit(solution)/shard_map/all_to_all | solution.py:366
  14.9 0.0 reduce-scatter.3.cloned.1.call-start
  14.9 7.5 %copy.42 = bf16[512,2,3,1024]{3,0,2,1:T(8,128)(2,1)} copy(bf16[512,2,3,1024]{3,1,2,0:T(2,128)(2,1)} %param.6) | data formatting | bytes 12582912 | tf_op args[1]
  22.5 17.5 %all-to-all-done = bf16[256,8,512]{2,0,1:T(8,128)(2,1)S(1)} async-done(((bf16[256,8,512]{2,0,1:T(8,128)(2,1)}), bf16[256,8,512]{2,0,1:T(8,128)(2,1)S(1)}, u32[]{:S(2)}, u32[]{:S(2)}) %all-to-all-start) | async-done | bytes 2097184 | tf_op jit(solution)/shard_map/all_to_all | solution.py:366
  40.0 0.0 copy-start.2
  40.0 1.3 copy-done.2
  41.3 14.1 %project.1 = bf16[8,2048,384]{2,1,0:T(8,128)(2,1)} custom-call(s32[16]{0:T(128)} %mods_ref.3, bf16[2048,512]{1,0:T(8,128)(2,1)} %bitcast.36, bf16[2,3,512,1024]{3,2,1,0:T(8,128)(2,1)} %bitcast.33), custom_call_target="tpu_custom_call" | custom-call | tf_op jit(solution)/shard_map/project/pallas_call | solution.py:181
  55.4 0.0 reduce-scatter.3.cloned.1.call-update
  55.4 0.0 copy-done
  55.4 0.9 bitcast_bitcast_fusion
  56.3 5.0 %all-to-all-start.1 = ((bf16[8,256,128]{2,1,0:T(8,128)(2,1)}), bf16[8,256,128]{2,1,0:T(8,128)(2,1)S(1)}, u32[]{:S(2)}, u32[]{:S(2)}) async-start(bf16[8,256,128]{2,1,0:T(8,128)(2,1)} %bitcast_bitcast_fusion), calls=%async_computation.2 | async-start | bytes 1048576 | tf_op jit(solution)/shard_map/all_to_all | solution.py:367
  61.3 0.0 all-gather.2.cloned.1.call-start
  61.3 0.0 copy-done.6
  61.3 1.3 copy.31.col_ref
  62.7 6.9 %all-to-all-done.1 = bf16[8,256,128]{2,1,0:T(8,128)(2,1)S(1)} async-done(((bf16[8,256,128]{2,1,0:T(8,128)(2,1)}), bf16[8,256,128]{2,1,0:T(8,128)(2,1)S(1)}, u32[]{:S(2)}, u32[]{:S(2)}) %all-to-all-start.1) | async-done | bytes 524320 | tf_op jit(solution)/shard_map/all_to_all | solution.py:367
  69.5 78.4 %reduce-scatter.3.cloned.1.call-done.qkv_ref = bf16[1,2048,384]{2,1,0:T(8,128)(2,1)} async-done(((bf16[8,2048,384]{2,1,0:T(8,128)(2,1)}), bf16[1,2048,384]{2,1,0:T(8,128)(2,1)}) %reduce-scatter.3.cloned.1.call-update) | async-done | bytes 1572880 | tf_op jit(solution)/shard_map/reduce_scatter | solution.py:376
  147.9 0.0 copy-done.4
  147.9 20.7 %attention.1 = (bf16[1,2048,128]{2,1,0:T(8,128)(2,1)}, bf16[1,2048,384]{2,1,0:T(8,128)(2,1)}) custom-call(bf16[1,2048,384]{2,1,0:T(8,128)(2,1)} %reduce-scatter.3.cloned.1.call-done.qkv_ref, bf16[1,2048,128]{2,1,0:T(8,128)(2,1)} %bitcast.41, s32[2048,1]{1,0:T(8,128)} %copy.31.col_ref, s32[1,2048]{1,0:T(1,128)} %bitcast.42), custom_call_target="tpu_custom_call" | custom-call | tf_op jit(solution)/shard_map/attention/pallas_call | solution.py:243
  168.6 0.0 all-gather.2.cloned.1.call-update
  168.6 0.0 copy-start.7
  168.6 0.0 copy-start.3
  168.6 0.0 reduce-scatter.5.cloned.1.call-start
  168.7 72.8 %all-gather.2.cloned.1.call-done.d_ref = bf16[8,2048,384]{2,1,0:T(8,128)(2,1)} async-done(((bf16[1,2048,384]{2,1,0:T(8,128)(2,1)}), bf16[8,2048,384]{2,1,0:T(8,128)(2,1)}) %all-gather.2.cloned.1.call-update) | async-done | bytes 12582928 | tf_op jit(solution)/shard_map/all_gather | solution.py:382
  241.5 23.3 %input_parts.1 = bf16[2048,512]{1,0:T(8,128)(2,1)} custom-call(s32[16]{0:T(128)} %mods_ref.3, bf16[8,2048,384]{2,1,0:T(8,128)(2,1)} %all-gather.2.cloned.1.call-done.d_ref, bf16[2,3,512,1024]{3,2,1,0:T(8,128)(2,1)} %bitcast.34), custom_call_target="tpu_custom_call" | custom-call | tf_op jit(solution)/shard_map/input_parts/pallas_call | solution.py:296
  264.8 0.0 reduce-scatter.5.cloned.1.call-update
  264.9 0.0 copy-done.7
  264.9 0.1 broadcast_bitcast_fusion
  265.0 0.0 copy-done.3
  265.0 2.5 copy.34
  267.5 3.8 %all-to-all-start.2 = ((bf16[8,1,256,128]{3,2,1,0:T(8,128)(2,1)}), bf16[8,1,256,128]{3,2,1,0:T(8,128)(2,1)S(1)}, u32[]{:S(2)}, u32[]{:S(2)}) async-start(bf16[8,1,256,128]{3,2,1,0:T(8,128)(2,1)} %bitcast.8), calls=%async_computation.3 | async-start | bytes 1048576 | tf_op jit(solution)/shard_map/all_to_all | solution.py:379
  271.4 36.9 %reduce-scatter.5.cloned.1.call-done = bf16[512,512]{1,0:T(8,128)(2,1)} async-done(((bf16[2048,512]{1,0:T(8,128)(2,1)}), bf16[512,512]{1,0:T(8,128)(2,1)}) %reduce-scatter.5.cloned.1.call-update) | async-done | bytes 524304 | tf_op jit(solution)/shard_map/reduce_scatter | solution.py:341
  308.3 1.1 constant_dynamic-slice_fusion
  309.3 2.1 collective-permute-start
  311.4 3.4 collective-permute-start.1
  314.9 3.9 %broadcast_select_fusion.x_ref = bf16[2,512,2048]{2,1,0:T(8,128)(2,1)} fusion(pred[2,2048]{1,0:T(4,128)(4,1)S(1)} %iota_compare_fusion, bf16[512,2048]{1,0:T(8,128)(2,1)} %copy.34), kind=kLoop, calls=%fused_computation.1 | loop fusion | flops 2097152 | bytes 6295552 | tf_op jit(solution)/shard_map/jit(_where)/select_n | solution.py:386
  318.8 0.0 all-to-all-done.2
  318.8 0.2 copy.33
  319.0 1.0 copy.35
  320.0 18.1 %weight_grads.1 = bf16[2,3,512,1024]{3,2,1,0:T(8,128)(2,1)} custom-call(bf16[8,2048,384]{2,1,0:T(8,128)(2,1)} %all-gather.2.cloned.1.call-done.d_ref, bf16[2,512,2048]{2,1,0:T(8,128)(2,1)} %broadcast_select_fusion.x_ref), custom_call_target="tpu_custom_call" | custom-call | tf_op jit(solution)/shard_map/weight_grads/pallas_call | solution.py:324
  338.1 12.7 %copy.36 = bf16[512,2,3,1024]{3,1,2,0:T(2,128)(2,1)} copy(bf16[512,2,3,1024]{3,0,2,1:T(8,128)(2,1)} %bitcast.35) | data formatting | bytes 12582912
  350.8 0.0 collective-permute-done
  350.8 0.1 broadcast_in_dim.40
  350.9 0.0 collective-permute-done.1
  351.0 0.0 copy-start.5
  351.0 0.8 copy-done.5
  351.8 0.0 copy-done.1
  (6 shorter events, 0.1 us)
Async XLA Ops:
  7.2 48.3 %copy-start = (bf16[256,1024]{1,0:T(8,128)(2,1)S(1)}, bf16[256,1024]{1,0:T(8,128)(2,1)}, u32[]{:S(2)}) copy-start(bf16[256,1024]{1,0:T(8,128)(2,1)} %param.9) | copy-start | bytes 1572868
  10.4 29.6 %all-to-all-start = ((bf16[256,8,512]{2,0,1:T(8,128)(2,1)}), bf16[256,8,512]{2,0,1:T(8,128)(2,1)S(1)}, u32[]{:S(2)}, u32[]{:S(2)}) async-start(bf16[256,8,512]{2,0,1:T(8,128)(2,1)} %bitcast.38), calls=%async_computation | async-start | bytes 4194304 | tf_op jit(solution)/shard_map/all_to_all | solution.py:366
  14.9 133.0 %reduce-scatter.3.cloned.1.call-start = ((), (), s32[]{:S(2)}) async-start(), calls=%async_computation.5 | async-start | bytes 14155776 | tf_op jit(solution)/shard_map/reduce_scatter | solution.py:376
  40.0 1.3 copy-start.2
  55.4 5.9 %copy-start.6 = (s32[2048]{0:T(1024)S(1)}, s32[2048]{0:T(1024)}, u32[]{:S(2)}) copy-start(s32[2048]{0:T(1024)} %param.8) | copy-start | bytes 24580
  56.3 13.2 %all-to-all-start.1 = ((bf16[8,256,128]{2,1,0:T(8,128)(2,1)}), bf16[8,256,128]{2,1,0:T(8,128)(2,1)S(1)}, u32[]{:S(2)}, u32[]{:S(2)}) async-start(bf16[8,256,128]{2,1,0:T(8,128)(2,1)} %bitcast_bitcast_fusion), calls=%async_computation.2 | async-start | bytes 1048576 | tf_op jit(solution)/shard_map/all_to_all | solution.py:367
  61.3 180.2 %all-gather.2.cloned.1.call-start = ((), (), s32[]{:S(2)}) async-start(), calls=%async_computation.6 | async-start | bytes 14155776 | tf_op jit(solution)/shard_map/all_gather | solution.py:382
  69.5 78.4 %copy-start.4 = (bf16[8,256,128]{2,1,0:T(8,128)(2,1)}, bf16[8,256,128]{2,1,0:T(8,128)(2,1)S(1)}, u32[]{:S(2)}) copy-start(bf16[8,256,128]{2,1,0:T(8,128)(2,1)S(1)} %all-to-all-done.1) | copy-start | bytes 1572868
  168.6 96.3 %copy-start.7 = (s32[16]{0:T(128)S(1)}, s32[16]{0:T(128)}, u32[]{:S(2)}) copy-start(s32[16]{0:T(128)} %mods_ref.3) | copy-start | bytes 196
  168.6 96.4 %copy-start.3 = (bf16[256,8,512]{2,0,1:T(8,128)(2,1)S(1)}, bf16[256,8,512]{2,0,1:T(8,128)(2,1)}, u32[]{:S(2)}) copy-start(bf16[256,8,512]{2,0,1:T(8,128)(2,1)} %copy-done.2) | copy-start | bytes 6291460
  168.6 139.6 %reduce-scatter.5.cloned.1.call-start = ((), (), s32[]{:S(2)}) async-start(), calls=%async_computation.7 | async-start | bytes 2621440 | tf_op jit(solution)/shard_map/reduce_scatter | solution.py:341
  267.5 51.3 %all-to-all-start.2 = ((bf16[8,1,256,128]{3,2,1,0:T(8,128)(2,1)}), bf16[8,1,256,128]{3,2,1,0:T(8,128)(2,1)S(1)}, u32[]{:S(2)}, u32[]{:S(2)}) async-start(bf16[8,1,256,128]{3,2,1,0:T(8,128)(2,1)} %bitcast.8), calls=%async_computation.3 | async-start | bytes 1048576 | tf_op jit(solution)/shard_map/all_to_all | solution.py:379
  309.3 41.5 %collective-permute-start = (bf16[256,512]{1,0:T(8,128)(2,1)S(1)}, bf16[256,512]{1,0:T(8,128)(2,1)S(1)}, u32[]{:S(2)}, u32[]{:S(2)}) collective-permute-start(bf16[256,512]{1,0:T(8,128)(2,1)S(1)} %get-tuple-element.20), channel_id=1, source_target_pairs={{0,0},{1,8},{2,16},{3,24},{4,4},{5,12},{6,20},{7,28},{8,1},{9,9},{... | collective-permute-start | bytes 786440 | tf_op jit(solution)/shard_map/ppermute | solution.py:352
  311.4 39.5 %collective-permute-start.1 = (bf16[256,512]{1,0:T(8,128)(2,1)S(1)}, bf16[256,512]{1,0:T(8,128)(2,1)S(1)}, u32[]{:S(2)}, u32[]{:S(2)}) collective-permute-start(bf16[256,512]{1,0:T(8,128)(2,1)S(1)} %get-tuple-element.19), channel_id=1, source_target_pairs={{0,4},{1,12},{2,20},{3,28},{4,0},{5,8},{6,16},{7,24},{8,5},{9,13},... | collective-permute-start | bytes 786440 | tf_op jit(solution)/shard_map/ppermute | solution.py:352
  338.1 13.7 %copy-start.1 = (bf16[256,1024]{1,0:T(8,128)(2,1)S(1)}, bf16[256,1024]{1,0:T(8,128)(2,1)}, u32[]{:S(2)}) copy-start(bf16[256,1024]{1,0:T(8,128)(2,1)} %param.9) | copy-start | bytes 1572868
  351.0 0.8 copy-start.5
Sparse Core Ops, SparseCore 0:
  55.5 92.3 reduce-scatter.2
  168.7 72.6 all-gather.1
  265.0 43.2 reduce-scatter.4

commit v2 on v1

--- a/solution.py
+++ b/solution.py
@@ -159,43 +159,71 @@
     return pltpu.CompilerParams(vmem_limit_bytes=VMEM_LIMIT)
 
 
-def project_kernel(pair, mods_ref, x_ref, w_ref, out_ref):
-    blocks = x_ref.shape[0] // BLOCK
-
-    def one(b, carry):
-        rows = pl.ds(pl.multiple_of(b * BLOCK, BLOCK), BLOCK)
-        x = x_ref[rows, :]
-        modality = mods_ref[b]
+def cost(flops, moved):
+    return pl.CostEstimate(flops=int(flops), bytes_accessed=int(moved), transcendentals=0)
+
+
+def pair_blocks(mods):
+    count = mods.shape[0]
+    slots = jnp.arange(2 * (count // 2 + 1), dtype=jnp.int32)
+    is_text = (mods == 0).astype(jnp.int32)
+    texts = jnp.sum(is_text)
+    index = jnp.arange(count, dtype=jnp.int32)
+    before = (mods[None, :] == mods[:, None]) & (index[None, :] < index[:, None])
+    rank = jnp.sum(before.astype(jnp.int32), axis=1)
+    spot = jnp.where(mods == 0, rank, 2 * ((texts + 1) // 2) + rank)
+    hit = spot[None, :] == slots[:, None]
+    block = jnp.sum(jnp.where(hit, jnp.arange(count, dtype=jnp.int32)[None, :], 0), axis=1)
+    pairs = block.reshape(-1, 2)
+    full = jnp.any(hit, axis=1).reshape(-1, 2)
+    second = jnp.where(full[:, 1], pairs[:, 1], pairs[:, 0])
+    number = (texts + 1) // 2 + (count - texts + 1) // 2
+    return jnp.stack([pairs[:, 0], second], 1).reshape(-1), number[None].astype(jnp.int32)
+
+
+def block_rows(b):
+    return pl.ds(pl.multiple_of(b * BLOCK, BLOCK), BLOCK)
+
+
+def project_kernel(pair, mods_ref, order_ref, number_ref, x_ref, w_ref, out_ref):
+    def one(n, carry):
+        first, second = order_ref[2 * n], order_ref[2 * n + 1]
+        x = jnp.concatenate([x_ref[block_rows(first), :], x_ref[block_rows(second), :]], axis=0)
+        modality = mods_ref[first]
         for p in range(3):
             y = dot_f32(x, w_ref[modality, p]).astype(jnp.bfloat16)
             for h in range(pair):
-                out_ref[h, rows, p * HD : (p + 1) * HD] = y[:, h * HD : (h + 1) * HD]
+                part = y[:, h * HD : (h + 1) * HD]
+                out_ref[h, block_rows(first), p * HD : (p + 1) * HD] = part[:BLOCK]
+                out_ref[h, block_rows(second), p * HD : (p + 1) * HD] = part[BLOCK:]
         return carry
 
-    lax.fori_loop(0, blocks, one, 0, unroll=4)
+    lax.fori_loop(0, number_ref[0], one, 0)
 
 
 def project(columns, planes, block_modality, pair):
     rows, width = columns.shape
     heads = planes.shape[3] // HD
+    order, number = pair_blocks(block_modality)
     return pl.pallas_call(
         functools.partial(project_kernel, pair),
         out_shape=jax.ShapeDtypeStruct((heads, rows, 3 * HD), jnp.bfloat16),
         grid_spec=pltpu.PrefetchScalarGridSpec(
-            num_scalar_prefetch=1,
+            num_scalar_prefetch=3,
             grid=(heads // pair,),
             in_specs=[
-                pl.BlockSpec((rows, width), lambda h, m: (0, 0)),
-                pl.BlockSpec((2, 3, width, pair * HD), lambda h, m: (0, 0, 0, h)),
+                pl.BlockSpec((rows, width), lambda h, *_: (0, 0)),
+                pl.BlockSpec((2, 3, width, pair * HD), lambda h, *_: (0, 0, 0, h)),
             ],
-            out_specs=pl.BlockSpec((pair, rows, 3 * HD), lambda h, m: (h, 0, 0)),
+            out_specs=pl.BlockSpec((pair, rows, 3 * HD), lambda h, *_: (h, 0, 0)),
         ),
         compiler_params=params(),
+        cost_estimate=cost(6 * rows * width * heads * HD, 6 * rows * heads * HD),
         name="project",
-    )(block_modality, columns, planes)
-
-
-def attention_kernel(step, window, qkv_ref, g_ref, col_ref, row_ref, att_ref, grad_ref, dk_acc, dv_acc):
+    )(block_modality, order, number, columns, planes)
+
+
+def attention_kernel(step, window, chunks, qkv_ref, g_ref, col_ref, row_ref, att_ref, grad_ref, dk_acc, dv_acc):
     i = pl.program_id(1)
     scale = HD ** (-0.5)
     low = pl.multiple_of(jnp.maximum((i + 1) * step - window, 0), step)
@@ -225,26 +253,31 @@
     dprob = dot_f32(g, v, NT)
     delta = jnp.sum(probs_f * dprob, axis=1, keepdims=True)
     dscore = (probs_f * (dprob - delta)).astype(jnp.bfloat16)
-    grad_ref[0, mine, 0:HD] = (dot_f32(dscore, k) * scale).astype(jnp.bfloat16)
+    place = pl.ds(pl.multiple_of((i // chunks) * step, step), step)
+    grad_ref[0, lax.rem(i, chunks), place, 0:HD] = (dot_f32(dscore, k) * scale).astype(jnp.bfloat16)
     dk_acc[seen, :] += dot_f32(dscore, q, TN)
     dv_acc[seen, :] += dot_f32(probs, g, TN)
 
     @pl.when(i == pl.num_programs(1) - 1)
     def _():
-        grad_ref[0, :, HD : 2 * HD] = (dk_acc[...] * scale).astype(jnp.bfloat16)
-        grad_ref[0, :, 2 * HD : 3 * HD] = dv_acc[...].astype(jnp.bfloat16)
-
-
-def attention(qkv, upstream, doc_ids, step):
+        for block in range(dk_acc.shape[0] // step):
+            rows = slice(block * step, (block + 1) * step)
+            chunk, at = block % chunks, (block // chunks) * step
+            spot = slice(at, at + step)
+            grad_ref[0, chunk, spot, HD : 2 * HD] = (dk_acc[rows, :] * scale).astype(jnp.bfloat16)
+            grad_ref[0, chunk, spot, 2 * HD : 3 * HD] = dv_acc[rows, :].astype(jnp.bfloat16)
+
+
+def attention(qkv, upstream, doc_ids, step, chunks):
     heads, rows, width = qkv.shape
     window = min((SPAN + 1) * step, rows)
     whole = lambda h, i: (h, 0, 0)
     fixed = lambda h, i: (0, 0)
     return pl.pallas_call(
-        functools.partial(attention_kernel, step, window),
+        functools.partial(attention_kernel, step, window, chunks),
         out_shape=(
             jax.ShapeDtypeStruct((heads, rows, HD), jnp.bfloat16),
-            jax.ShapeDtypeStruct((heads, rows, width), jnp.bfloat16),
+            jax.ShapeDtypeStruct((heads, chunks, rows // chunks, width), jnp.bfloat16),
         ),
         grid=(heads, rows // step),
         in_specs=[
@@ -255,100 +288,111 @@
         ],
         out_specs=[
             pl.BlockSpec((1, rows, HD), whole),
-            pl.BlockSpec((1, rows, width), whole),
+            pl.BlockSpec((1, chunks, rows // chunks, width), lambda h, i: (h, 0, 0, 0)),
         ],
+        cost_estimate=cost(10 * heads * rows * window * HD, 16 * heads * rows * HD),
         scratch_shapes=[pltpu.VMEM((rows, HD), jnp.float32)] * 2,
         compiler_params=params(),
         name="attention",
     )(qkv, upstream, doc_ids[:, None], doc_ids[None, :])
 
 
-def input_kernel(pair, mods_ref, d_ref, w_ref, out_ref, acc):
+def input_kernel(pair, mods_ref, order_ref, number_ref, d_ref, w_ref, out_ref, acc):
     step = pl.program_id(0)
-    blocks = d_ref.shape[1] // BLOCK
 
     @pl.when(step == 0)
     def _():
         acc[...] = jnp.zeros_like(acc)
 
-    def one(b, carry):
-        rows = pl.ds(pl.multiple_of(b * BLOCK, BLOCK), BLOCK)
-        modality = mods_ref[b]
-        total = acc[rows, :]
+    def one(n, carry):
+        first, second = block_rows(order_ref[2 * n]), block_rows(order_ref[2 * n + 1])
+        modality = mods_ref[order_ref[2 * n]]
+        total = jnp.concatenate([acc[first, :], acc[second, :]], axis=0)
         for p in range(3):
-            lhs = jnp.concatenate(
-                [d_ref[h, rows, p * HD : (p + 1) * HD] for h in range(pair)], axis=1
-            )
-            total = total + dot_f32(lhs, w_ref[modality, p], NT)
-        acc[rows, :] = total
+            parts = [
+                jnp.concatenate([d_ref[h, r, p * HD : (p + 1) * HD] for r in (first, second)], axis=0)
+                for h in range(pair)
+            ]
+            total = total + dot_f32(jnp.concatenate(parts, axis=1), w_ref[modality, p], NT)
+        acc[first, :] = total[:BLOCK]
+        acc[second, :] = total[BLOCK:]
         return carry
 
-    lax.fori_loop(0, blocks, one, 0, unroll=4)
+    lax.fori_loop(0, number_ref[0], one, 0)
 
     @pl.when(step == pl.num_programs(0) - 1)
     def _():
         out_ref[...] = acc[...].astype(jnp.bfloat16)
 
 
-def input_parts(grads, planes, block_modality, pair):
+def input_parts(grads, planes, mods, pair):
     heads, rows, width3 = grads.shape
     width = planes.shape[2]
+    order, number = pair_blocks(mods)
     return pl.pallas_call(
         functools.partial(input_kernel, pair),
         out_shape=jax.ShapeDtypeStruct((rows, width), jnp.bfloat16),
         grid_spec=pltpu.PrefetchScalarGridSpec(
-            num_scalar_prefetch=1,
+            num_scalar_prefetch=3,
             grid=(heads // pair,),
             in_specs=[
-                pl.BlockSpec((pair, rows, width3), lambda h, m: (h, 0, 0)),
-                pl.BlockSpec((2, 3, width, pair * HD), lambda h, m: (0, 0, 0, h)),
+                pl.BlockSpec((pair, rows, width3), lambda h, *_: (h, 0, 0)),
+                pl.BlockSpec((2, 3, width, pair * HD), lambda h, *_: (0, 0, 0, h)),
             ],
-            out_specs=pl.BlockSpec((rows, width), lambda h, m: (0, 0)),
+            out_specs=pl.BlockSpec((rows, width), lambda h, *_: (0, 0)),
             scratch_shapes=[pltpu.VMEM((rows, width), jnp.float32)],
         ),
         compiler_params=params(),
+        cost_estimate=cost(6 * rows * width * heads * HD, 6 * rows * heads * HD),
         name="input_parts",
-    )(block_modality, grads, planes)
-
-
-def weight_kernel(pair, d_ref, x_ref, out_ref):
+    )(mods, order, number, grads, planes)
+
+
+def weight_kernel(pair, x_ref, *refs):
+    d_refs, out_ref = refs[:-1], refs[-1]
+    rows = d_refs[0].shape[1]
     for p in range(3):
-        rhs = jnp.concatenate([d_ref[h, :, p * HD : (p + 1) * HD] for h in range(pair)], axis=1)
+        cols = slice(p * HD, (p + 1) * HD)
+        rhs = [jnp.concatenate([d[h, :, cols] for h in range(pair)], axis=1) for d in d_refs]
         for modality in range(2):
-            out_ref[modality, p] = dot_f32(x_ref[modality], rhs).astype(jnp.bfloat16)
-
-
-def weight_grads(grads, flipped, pair):
-    heads, rows, width3 = grads.shape
-    width = flipped.shape[1]
+            total = dot_f32(x_ref[modality, :, 0:rows], rhs[0])
+            for c in range(1, len(rhs)):
+                total = total + dot_f32(x_ref[modality, :, c * rows : (c + 1) * rows], rhs[c])
+            out_ref[modality, p] = total.astype(jnp.bfloat16)
+
+
+def weight_grads(gathered, flipped, pair):
+    heads, rows, width3 = gathered[0].shape
+    width, total_rows = flipped.shape[1:]
     return pl.pallas_call(
         functools.partial(weight_kernel, pair),
         out_shape=jax.ShapeDtypeStruct((2, 3, width, heads * HD), jnp.bfloat16),
         grid=(heads // pair,),
-        in_specs=[
-            pl.BlockSpec((pair, rows, width3), lambda h: (h, 0, 0)),
-            pl.BlockSpec((2, width, rows), lambda h: (0, 0, 0)),
-        ],
+        in_specs=[pl.BlockSpec((2, width, total_rows), lambda h: (0, 0, 0))]
+        + [pl.BlockSpec((pair, rows, width3), lambda h: (h, 0, 0))] * len(gathered),
         out_specs=pl.BlockSpec((2, 3, width, pair * HD), lambda h: (0, 0, 0, h)),
         compiler_params=params(),
+        cost_estimate=cost(12 * total_rows * width * heads * HD, 6 * total_rows * heads * HD),
         name="weight_grads",
-    )(grads, flipped)
-
-
-def place_inputs(parts):
+    )(flipped, *gathered)
+
+
+def place_inputs(sums):
     dp, mp = lax.axis_size("dp"), lax.axis_size("mp")
-    ratio = dp // mp
-    summed = lax.psum_scatter(parts, "mp", scatter_dimension=0, tiled=True)
-    rows, width = summed.shape[0] // ratio, summed.shape[1]
+    ratio = len(sums)
+    rows, width = sums[0].shape
     mine = lax.axis_index("dp")
-    placed = jnp.zeros((rows, ratio * width), summed.dtype)
+    placed = jnp.zeros((rows, ratio * width), sums[0].dtype)
     for s in range(ratio):
         route = [
             (j * mp + g, (ratio * g + (j + s) % ratio) * mp + j // ratio)
             for j in range(dp)
             for g in range(mp)
         ]
-        sent = lax.dynamic_slice_in_dim(summed, ((mine + s) % ratio) * rows, rows, 0)
+        chosen = (mine + s) % ratio
+        sent = sums[0]
+        for c in range(1, ratio):
+            sent = jnp.where(chosen == c, sums[c], sent)
         piece = lax.ppermute(sent, ("dp", "mp"), route)
         spot = (mine - s + ratio) % ratio
         placed = lax.dynamic_update_slice_in_dim(placed, piece, spot * width, 1)
@@ -372,21 +416,41 @@
         tiled=True,
     )
     planes = jnp.transpose(weights, (1, 2, 0, 3))
+    columns, upstream = lax.optimization_barrier((columns, upstream))
+    mp = lax.axis_size("mp")
+    chunks = dp // mp
+    chunk_rows = total_rows // chunks
+    dp_mods = block_modality.reshape(mp, chunks, local_rows // BLOCK)
     partial = project(columns, planes, block_modality, pair)
-    qkv = lax.psum_scatter(partial, "dp", scatter_dimension=0, tiled=True)
-    attended, grads = attention(qkv, upstream, doc_ids, local_rows)
+    qkv = lax.psum_scatter(
+        partial.reshape(heads * total_rows, 3 * HD), "dp", scatter_dimension=0, tiled=True
+    )
+    token_mods = jnp.broadcast_to(
+        dp_mods.transpose(1, 0, 2)[..., None], (chunks, mp, local_rows // BLOCK, BLOCK)
+    ).reshape(total_rows)
+    shuffled = columns.reshape(mp, chunks, local_rows, columns.shape[1]).transpose(1, 0, 2, 3)
+    shuffled = shuffled.reshape(total_rows, columns.shape[1])
+    mask = token_mods[None, :] == jnp.arange(2, dtype=jnp.int32)[:, None]
+    flipped = jnp.where(mask[:, None, :], shuffled.T[None], jnp.zeros((), jnp.bfloat16))
+    qkv, flipped = lax.optimization_barrier((qkv, flipped))
+    qkv = qkv.reshape(own, total_rows, 3 * HD)
+    attended, grads = attention(qkv, upstream, doc_ids, local_rows, chunks)
+    gathered, sums = [], []
+    for c in range(chunks):
+        flat = grads[:, c].reshape(own * chunk_rows, 3 * HD)
+        whole = lax.all_gather(flat, "dp", axis=0, tiled=True)
+        gathered.append(whole.reshape(heads, chunk_rows, 3 * HD))
+    for c in range(chunks):
+        parts = input_parts(gathered[c], planes, dp_mods[:, c].reshape(-1), pair)
+        sums.append(lax.psum_scatter(parts, "mp", scatter_dimension=0, tiled=True))
     attended = attended.reshape(own, dp, local_rows, HD).transpose(1, 0, 2, 3)
     attended = lax.all_to_all(attended, "dp", split_axis=0, concat_axis=0, tiled=True)
     attended = attended.reshape(heads, local_rows, HD)
     attended = attended.transpose(1, 0, 2).reshape(local_rows, head_width)
-    gathered = lax.all_gather(grads, "dp", axis=0, tiled=True)
-    token_mods = jnp.broadcast_to(block_modality[:, None], (total_rows // BLOCK, BLOCK))
-    token_mods = token_mods.reshape(total_rows)
-    mask = token_mods[None, :] == jnp.arange(2, dtype=jnp.int32)[:, None]
-    flipped = jnp.where(mask[:, None, :], columns.T[None], jnp.zeros((), jnp.bfloat16))
-    parts = input_parts(gathered, planes, block_modality, pair)
-    grad_tokens = place_inputs(parts)
-    grad_weights = jnp.transpose(weight_grads(gathered, flipped, pair), (2, 0, 1, 3))
+    by_plane = weight_grads(gathered, flipped, pair)
+    by_plane, *sums = lax.optimization_barrier((by_plane, *sums))
+    grad_tokens = place_inputs(sums)
+    grad_weights = jnp.transpose(by_plane, (2, 0, 1, 3))
     return attended, grad_tokens, grad_weights
 
 

time: 362 us -> 387 us (1.069)
  local copies, waits for them, and re-layouts: 32.8 us -> 42.6 us
  waiting for transfers between devices: 213 us -> 219 us
  Pallas kernels: 76.2 us -> 80.5 us
  between operations: 13.9 us -> 17.8 us
    ppermute x2, waiting for transfers between devices: 0.01 us -> 19.5 us  [place_inputs(): piece = lax.ppermute(sent, ('dp', 'mp'), route)]
    reduce_scatter x2 -> x3, waiting for transfers between devices: 115 us -> 104 us  [the longest x1 80.9 us: by_heads(): lax.psum_scatter(partial.reshape(heads * total_rows, 3 * HD), 'dp', scatt...]
    reshape x0 -> x11, local copies, waits for them, and re-layouts: none -> 5.77 us  [the longest x1 3.36 us: by_heads(): shuffled = shuffled.reshape(total_rows, columns.shape[1])]
    pallas_call x1, Pallas kernels: 14.1 us -> 19 us  [project(): pl.pallas_call(functools.partial(project_kernel, pair), out_shape=jax.Sha...]
    all_gather x1 -> x2, waiting for transfers between devices: 72.8 us -> 76.3 us  [by_heads(): whole = lax.all_gather(flat, 'dp', axis=0, tiled=True)]
    unnamed x19 -> x25, local copies, waits for them, and re-layouts: 23.4 us -> 25 us
    pallas_call x1 -> x2, Pallas kernels: 23.3 us -> 22.7 us  [input_parts(): pl.pallas_call(functools.partial(input_kernel, pair), out_shape=jax.Shape...]
  transfers between devices with their start and end apart: 8 -> 10, of which waited for: 5 -> 8; matrix products, arithmetic and copies ran while one was open for 9% -> 11% of each run, Pallas kernels for 5% -> 11%
where the time goes in v2:
time: 387 us; the launch traced here: 386 us
  waiting for transfers between devices  219 us (57%)
  Pallas kernels  80.5 us (21%)
  local copies, waits for them, and re-layouts  42.6 us (11%)
  starting transfers between devices  19 us (5%)
  between operations  17.8 us (5%)
  other arithmetic  6.82 us (2%)
    reduce_scatter x1, waiting for transfers between devices, by_heads(): lax.psum_scatter(partial.reshape(heads * total_rows, 3 * HD), 'dp', scatt...  80.9 us
    all_gather x2, waiting for transfers between devices, by_heads(): whole = lax.all_gather(flat, 'dp', axis=0, tiled=True)  76.3 us
    unnamed x25, local copies, waits for them, and re-layouts  25 us
    reduce_scatter x2, waiting for transfers between devices, by_heads(): sums.append(lax.psum_scatter(parts, 'mp', scatter_dimension=0, tiled=True))  22.7 us
    pallas_call x2, Pallas kernels, input_parts(): pl.pallas_call(functools.partial(input_kernel, pair), out_shape=jax.Shape...  22.7 us
    pallas_call x1, Pallas kernels, attention(): pl.pallas_call(functools.partial(attention_kernel, step, window, chunks),...  20.7 us
    ppermute x2, waiting for transfers between devices, place_inputs(): piece = lax.ppermute(sent, ('dp', 'mp'), route)  19.5 us
    pallas_call x1, Pallas kernels, project(): pl.pallas_call(functools.partial(project_kernel, pair), out_shape=jax.Sha...  19 us
  transfers between devices with their start and end apart: 10, of which 8 were waited for; matrix products, arithmetic and copies ran while one was open for 11% of the time, Pallas kernels for 11%

profile of v2, /device:TPU:3, one launch (start us, length us, event | category | flops | bytes accessed | tf_op | source)
XLA Modules:
  0.0 386.2 jit_solution(15012745228669111586)
XLA Ops:
  7.2 1.0 copy-done
  8.2 0.9 bitcast_bitcast_fusion
  9.1 4.6 %all-to-all-start.1 = ((bf16[8,256,128]{2,1,0:T(8,128)(2,1)}), bf16[8,256,128]{2,1,0:T(8,128)(2,1)S(1)}, u32[]{:S(2)}, u32[]{:S(2)}) async-start(bf16[8,256,128]{2,1,0:T(8,128)(2,1)} %bitcast_bitcast_fusion), calls=%async_computation.1 | async-start | bytes 1048576 | tf_op jit(solution)/shard_map/all_to_all | solution.py:411
  13.7 3.2 copy.75
  16.8 5.0 %all-to-all-done.1 = bf16[8,256,128]{2,1,0:T(8,128)(2,1)S(1)} async-done(((bf16[8,256,128]{2,1,0:T(8,128)(2,1)}), bf16[8,256,128]{2,1,0:T(8,128)(2,1)S(1)}, u32[]{:S(2)}, u32[]{:S(2)}) %all-to-all-start.1) | async-done | bytes 524320 | tf_op jit(solution)/shard_map/all_to_all | solution.py:411
  21.9 5.1 %all-to-all-start = ((bf16[256,8,512]{2,0,1:T(8,128)(2,1)}), bf16[256,8,512]{2,0,1:T(8,128)(2,1)S(1)}, u32[]{:S(2)}, u32[]{:S(2)}) async-start(bf16[256,8,512]{2,0,1:T(8,128)(2,1)} %bitcast.50), calls=%async_computation | async-start | bytes 4194304 | tf_op jit(solution)/shard_map/all_to_all | solution.py:410
  26.9 0.6 fusion.8
  28.9 0.2 convert_reduce_fusion
  29.1 0.1 select_reduce_fusion
  29.3 0.1 fusion
  29.4 0.1 reshape.117
  29.6 0.6 reshape.118.order_ref
  30.2 7.5 %copy.74 = bf16[512,2,3,1024]{3,0,2,1:T(8,128)(2,1)} copy(bf16[512,2,3,1024]{3,1,2,0:T(2,128)(2,1)} %param.6) | data formatting | bytes 12582912 | tf_op args[1]
  37.8 14.3 %all-to-all-done = bf16[256,8,512]{2,0,1:T(8,128)(2,1)S(1)} async-done(((bf16[256,8,512]{2,0,1:T(8,128)(2,1)}), bf16[256,8,512]{2,0,1:T(8,128)(2,1)S(1)}, u32[]{:S(2)}, u32[]{:S(2)}) %all-to-all-start) | async-done | bytes 2097184 | tf_op jit(solution)/shard_map/all_to_all | solution.py:410
  52.0 1.4 copy-done.2
  53.4 19.0 %project.1 = bf16[8,2048,384]{2,1,0:T(8,128)(2,1)} custom-call(s32[16]{0:T(128)} %mods_ref.1, s32[18]{0:T(128)} %reshape.118.order_ref, s32[1]{0:T(128)} %bitcast.number_ref, bf16[2048,512]{1,0:T(8,128)(2,1)} %bitcast.48, bf16[2,3,512,1024]{3,2,1,0:T(8,128)(2,1)} %bitcast.44), custom_call_target="tpu_custom_call" | custom-call | flops 6442450944 | bytes 12582912 | tf_op jit(solution)/shard_map/project/pallas_call | solution.py:208
  72.5 0.6 copy-done.10
  73.2 1.4 copy.64.col_ref
  74.7 3.1 copy.63
  77.8 3.4 reshape.123
  81.2 2.9 broadcast_select_fusion.x_ref
  84.1 80.9 %reduce-scatter.4.cloned.1.call-done = bf16[2048,384]{1,0:T(8,128)(2,1)} async-done(((bf16[16384,384]{1,0:T(8,128)(2,1)}), bf16[2048,384]{1,0:T(8,128)(2,1)}) %reduce-scatter.4.cloned.1.call-update) | async-done | bytes 1572880 | tf_op jit(solution)/shard_map/reduce_scatter | solution.py:425
  165.0 20.7 %attention.1 = (bf16[1,2048,128]{2,1,0:T(8,128)(2,1)}, bf16[1,2,1024,384]{3,2,1,0:T(8,128)(2,1)}) custom-call(bf16[1,2048,384]{2,1,0:T(8,128)(2,1)} %bitcast.64, bf16[1,2048,128]{2,1,0:T(8,128)(2,1)} %bitcast.59, s32[2048,1]{1,0:T(8,128)} %copy.64.col_ref, s32[1,2048]{1,0:T(1,128)} %bitcast.62), custom_call_target="tpu_custom_call" | custom-call | flops 3355443200 | bytes 4194304 | tf_op jit(solution)/shard_map/attention/pallas_call | solution.py:276
  185.6 2.7 fusion.9
  188.4 0.7 all-gather.5.cloned.1.call-update
  189.2 0.7 fusion.7
  191.9 0.2 convert_reduce_fusion.1
  192.1 0.2 convert_reduce_fusion.2
  192.5 0.1 reshape.133
  192.8 0.6 reshape.134.order_ref
  193.4 41.2 %all-gather.7.cloned.1.call-done = bf16[1,1,8192,384]{3,2,1,0:T(8,128)(2,1)} async-done(((bf16[1,1,1024,384]{3,2,1,0:T(8,128)(2,1)}), bf16[1,1,8192,384]{3,2,1,0:T(8,128)(2,1)}) %all-gather.7.cloned.1.call-update) | async-done | bytes 6291472 | tf_op jit(solution)/shard_map/all_gather | solution.py:441
  234.6 10.7 %input_parts.3 = bf16[1024,512]{1,0:T(8,128)(2,1)} custom-call(s32[8]{0:T(128)} %copy-done.8, s32[10]{0:T(128)} %reshape.134.order_ref, s32[1]{0:T(128)} %bitcast.23.number_ref, bf16[8,1024,384]{2,1,0:T(8,128)(2,1)} %bitcast.52, bf16[2,3,512,1024]{3,2,1,0:T(8,128)(2,1)} %bitcast.45), custom_call_target="tpu_custom_call" | custom-call | flops 3221225472 | bytes 6291456 | tf_op jit(solution)/shard_map/input_parts/pallas_call | solution.py:332
  246.2 0.1 reshape.130
  246.4 0.6 reshape.131.order_ref
  247.0 35.0 %all-gather.5.cloned.1.call-done = bf16[1,1,8192,384]{3,2,1,0:T(8,128)(2,1)} async-done(((bf16[1,1,1024,384]{3,2,1,0:T(8,128)(2,1)}), bf16[1,1,8192,384]{3,2,1,0:T(8,128)(2,1)}) %all-gather.5.cloned.1.call-update) | async-done | bytes 6291472 | tf_op jit(solution)/shard_map/all_gather | solution.py:441
  282.1 12.0 %input_parts.2 = bf16[1024,512]{1,0:T(8,128)(2,1)} custom-call(s32[8]{0:T(128)} %copy-done.7, s32[10]{0:T(128)} %reshape.131.order_ref, s32[1]{0:T(128)} %bitcast.22.number_ref, bf16[8,1024,384]{2,1,0:T(8,128)(2,1)} %bitcast.54, bf16[2,3,512,1024]{3,2,1,0:T(8,128)(2,1)} %bitcast.46), custom_call_target="tpu_custom_call" | custom-call | flops 3221225472 | bytes 6291456 | tf_op jit(solution)/shard_map/input_parts/pallas_call | solution.py:332
  294.1 3.9 %all-to-all-start.2 = ((bf16[8,1,256,128]{3,2,1,0:T(8,128)(2,1)}), bf16[8,1,256,128]{3,2,1,0:T(8,128)(2,1)S(1)}, u32[]{:S(2)}, u32[]{:S(2)}) async-start(bf16[8,1,256,128]{3,2,1,0:T(8,128)(2,1)} %bitcast.16), calls=%async_computation.3 | async-start | bytes 1048576 | tf_op jit(solution)/shard_map/all_to_all | solution.py:447
  298.0 18.1 %weight_grads.1 = bf16[2,3,512,1024]{3,2,1,0:T(8,128)(2,1)} custom-call(bf16[2,512,2048]{2,1,0:T(8,128)(2,1)} %broadcast_select_fusion.x_ref, bf16[8,1024,384]{2,1,0:T(8,128)(2,1)} %bitcast.55, bf16[8,1024,384]{2,1,0:T(8,128)(2,1)} %bitcast.53), custom_call_target="tpu_custom_call" | custom-call | flops 12884901888 | bytes 12582912 | tf_op jit(solution)/shard_map/weight_grads/pallas_call | solution.py:367
  316.1 22.7 %reduce-scatter.6.cloned.1.call-done = bf16[256,512]{1,0:T(8,128)(2,1)} async-done(((bf16[1024,512]{1,0:T(8,128)(2,1)}), bf16[256,512]{1,0:T(8,128)(2,1)}) %reduce-scatter.6.cloned.1.call-update) | async-done | bytes 262160 | tf_op jit(solution)/shard_map/reduce_scatter | solution.py:445
  338.9 1.1 broadcast_select_fusion.1
  339.9 1.9 collective-permute-start
  341.9 3.4 collective-permute-start.1
  345.3 0.2 copy.66
  345.5 1.0 copy.67
  346.5 12.7 %copy.68 = bf16[512,2,3,1024]{3,1,2,0:T(2,128)(2,1)} copy(bf16[512,2,3,1024]{3,0,2,1:T(8,128)(2,1)} %bitcast.56) | data formatting | bytes 12582912
  359.2 13.3 %collective-permute-done = bf16[256,512]{1,0:T(8,128)(2,1)S(1)} collective-permute-done((bf16[256,512]{1,0:T(8,128)(2,1)S(1)}, bf16[256,512]{1,0:T(8,128)(2,1)S(1)}, u32[]{:S(2)}, u32[]{:S(2)}) %collective-permute-start) | collective-permute-done | bytes 262176 | tf_op jit(solution)/shard_map/ppermute | solution.py:396
  372.6 6.3 %collective-permute-done.1 = bf16[256,512]{1,0:T(8,128)(2,1)S(1)} collective-permute-done((bf16[256,512]{1,0:T(8,128)(2,1)S(1)}, bf16[256,512]{1,0:T(8,128)(2,1)S(1)}, u32[]{:S(2)}, u32[]{:S(2)}) %collective-permute-start.1) | collective-permute-done | bytes 262176 | tf_op jit(solution)/shard_map/ppermute | solution.py:396
  378.9 0.8 copy-done.4
  (53 shorter events, 1.8 us)
Async XLA Ops:
  7.2 1.1 copy-start
  9.1 12.8 %all-to-all-start.1 = ((bf16[8,256,128]{2,1,0:T(8,128)(2,1)}), bf16[8,256,128]{2,1,0:T(8,128)(2,1)S(1)}, u32[]{:S(2)}, u32[]{:S(2)}) async-start(bf16[8,256,128]{2,1,0:T(8,128)(2,1)} %bitcast_bitcast_fusion), calls=%async_computation.1 | async-start | bytes 1048576 | tf_op jit(solution)/shard_map/all_to_all | solution.py:411
  13.7 13.3 %copy-start.9 = (s32[16]{0:T(128)S(1)}, s32[16]{0:T(128)}, u32[]{:S(2)}) copy-start(s32[16]{0:T(128)} %mods_ref.1) | copy-start | bytes 196
  21.9 15.9 %copy-start.5 = (bf16[8,256,128]{2,1,0:T(8,128)(2,1)}, bf16[8,256,128]{2,1,0:T(8,128)(2,1)S(1)}, u32[]{:S(2)}) copy-start(bf16[8,256,128]{2,1,0:T(8,128)(2,1)S(1)} %all-to-all-done.1) | copy-start | bytes 1572868
  21.9 30.1 %all-to-all-start = ((bf16[256,8,512]{2,0,1:T(8,128)(2,1)}), bf16[256,8,512]{2,0,1:T(8,128)(2,1)S(1)}, u32[]{:S(2)}, u32[]{:S(2)}) async-start(bf16[256,8,512]{2,0,1:T(8,128)(2,1)} %bitcast.50), calls=%async_computation | async-start | bytes 4194304 | tf_op jit(solution)/shard_map/all_to_all | solution.py:410
  26.9 138.1 %reduce-scatter.4.cloned.1.call-start = ((), (), s32[]{:S(2)}) async-start(), calls=%async_computation.6 | async-start | bytes 14155776 | tf_op jit(solution)/shard_map/reduce_scatter | solution.py:425
  52.0 1.4 copy-start.2
  72.4 0.7 copy-start.10
  72.4 0.7 copy-start.6
  72.4 2.3 copy-start.3
  72.4 162.2 %all-gather.7.cloned.1.call-start = ((), (), s32[]{:S(2)}) async-start(), calls=%async_computation.10 | async-start | bytes 7077888 | tf_op jit(solution)/shard_map/all_gather | solution.py:441
  188.4 93.7 %all-gather.5.cloned.1.call-start = ((), (), s32[]{:S(2)}) async-start(), calls=%async_computation.9 | async-start | bytes 7077888 | tf_op jit(solution)/shard_map/all_gather | solution.py:441
  189.1 127.0 %reduce-scatter.8.cloned.1.call-start = ((), (), s32[]{:S(2)}) async-start(), calls=%async_computation.8 | async-start | bytes 1310720 | tf_op jit(solution)/shard_map/reduce_scatter | solution.py:445
  191.8 42.8 %copy-start.8 = (s32[8]{0:T(128)}, s32[8]{0:T(128)S(1)}, u32[]{:S(2)}) copy-start(s32[8]{0:T(128)S(1)} %reshape_squeeze.15.mods_ref) | copy-start | bytes 100
  191.9 53.4 %copy-start.7 = (s32[8]{0:T(128)}, s32[8]{0:T(128)S(1)}, u32[]{:S(2)}) copy-start(s32[8]{0:T(128)S(1)} %reshape_squeeze.14.mods_ref) | copy-start | bytes 100
  245.3 93.6 %reduce-scatter.6.cloned.1.call-start = ((), (), s32[]{:S(2)}) async-start(), calls=%async_computation.7 | async-start | bytes 1310720 | tf_op jit(solution)/shard_map/reduce_scatter | solution.py:445
  294.1 51.2 %all-to-all-start.2 = ((bf16[8,1,256,128]{3,2,1,0:T(8,128)(2,1)}), bf16[8,1,256,128]{3,2,1,0:T(8,128)(2,1)S(1)}, u32[]{:S(2)}, u32[]{:S(2)}) async-start(bf16[8,1,256,128]{3,2,1,0:T(8,128)(2,1)} %bitcast.16), calls=%async_computation.3 | async-start | bytes 1048576 | tf_op jit(solution)/shard_map/all_to_all | solution.py:447
  339.9 32.6 %collective-permute-start = (bf16[256,512]{1,0:T(8,128)(2,1)S(1)}, bf16[256,512]{1,0:T(8,128)(2,1)S(1)}, u32[]{:S(2)}, u32[]{:S(2)}) collective-permute-start(bf16[256,512]{1,0:T(8,128)(2,1)S(1)} %get-tuple-element.43), channel_id=1, source_target_pairs={{0,0},{1,8},{2,16},{3,24},{4,4},{5,12},{6,20},{7,28},{8,1},{9,9},{... | collective-permute-start | bytes 786440 | tf_op jit(solution)/shard_map/ppermute | solution.py:396
  341.9 37.0 %collective-permute-start.1 = (bf16[256,512]{1,0:T(8,128)(2,1)S(1)}, bf16[256,512]{1,0:T(8,128)(2,1)S(1)}, u32[]{:S(2)}, u32[]{:S(2)}) collective-permute-start(bf16[256,512]{1,0:T(8,128)(2,1)S(1)} %get-tuple-element.42), channel_id=1, source_target_pairs={{0,4},{1,12},{2,20},{3,28},{4,0},{5,8},{6,16},{7,24},{8,5},{9,13},... | collective-permute-start | bytes 786440 | tf_op jit(solution)/shard_map/ppermute | solution.py:396
  346.5 33.2 %copy-start.1 = (bf16[256,1024]{1,0:T(8,128)(2,1)S(1)}, bf16[256,1024]{1,0:T(8,128)(2,1)}, u32[]{:S(2)}) copy-start(bf16[256,1024]{1,0:T(8,128)(2,1)} %param.9) | copy-start | bytes 1572868
  378.9 0.8 copy-start.4
Sparse Core Ops, SparseCore 0:
  72.6 92.3 reduce-scatter.3
  188.5 46.0 all-gather.6
  236.5 45.5 all-gather.4
  284.2 26.5 reduce-scatter.7
  313.1 25.7 reduce-scatter.5

commit v3 on v2

--- a/solution.py
+++ b/solution.py
@@ -185,7 +185,16 @@
     return pl.ds(pl.multiple_of(b * BLOCK, BLOCK), BLOCK)
 
 
-def project_kernel(pair, mods_ref, order_ref, number_ref, x_ref, w_ref, out_ref):
+def columns_of(i, p):
+    return pl.ds(pl.multiple_of(i * (3 * HD) + p * HD, HD), HD)
+
+
+def spot_of(b, step, p):
+    per = step // BLOCK
+    return block_rows(lax.rem(b, per)), columns_of(b // per, p)
+
+
+def project_kernel(step, pair, mods_ref, order_ref, number_ref, x_ref, w_ref, out_ref):
     def one(n, carry):
         first, second = order_ref[2 * n], order_ref[2 * n + 1]
         x = jnp.concatenate([x_ref[block_rows(first), :], x_ref[block_rows(second), :]], axis=0)
@@ -194,20 +203,20 @@
             y = dot_f32(x, w_ref[modality, p]).astype(jnp.bfloat16)
             for h in range(pair):
                 part = y[:, h * HD : (h + 1) * HD]
-                out_ref[h, block_rows(first), p * HD : (p + 1) * HD] = part[:BLOCK]
-                out_ref[h, block_rows(second), p * HD : (p + 1) * HD] = part[BLOCK:]
+                out_ref[(h, *spot_of(first, step, p))] = part[:BLOCK]
+                out_ref[(h, *spot_of(second, step, p))] = part[BLOCK:]
         return carry
 
     lax.fori_loop(0, number_ref[0], one, 0)
 
 
-def project(columns, planes, block_modality, pair):
+def project(columns, planes, block_modality, pair, step):
     rows, width = columns.shape
     heads = planes.shape[3] // HD
     order, number = pair_blocks(block_modality)
     return pl.pallas_call(
-        functools.partial(project_kernel, pair),
-        out_shape=jax.ShapeDtypeStruct((heads, rows, 3 * HD), jnp.bfloat16),
+        functools.partial(project_kernel, step, pair),
+        out_shape=jax.ShapeDtypeStruct((heads, step, rows // step * 3 * HD), jnp.bfloat16),
         grid_spec=pltpu.PrefetchScalarGridSpec(
             num_scalar_prefetch=3,
             grid=(heads // pair,),
@@ -215,7 +224,7 @@
                 pl.BlockSpec((rows, width), lambda h, *_: (0, 0)),
                 pl.BlockSpec((2, 3, width, pair * HD), lambda h, *_: (0, 0, 0, h)),
             ],
-            out_specs=pl.BlockSpec((pair, rows, 3 * HD), lambda h, *_: (h, 0, 0)),
+            out_specs=pl.BlockSpec((pair, step, rows // step * 3 * HD), lambda h, *_: (h, 0, 0)),
         ),
         compiler_params=params(),
         cost_estimate=cost(6 * rows * width * heads * HD, 6 * rows * heads * HD),
@@ -223,7 +232,7 @@
     )(block_modality, order, number, columns, planes)
 
 
-def attention_kernel(step, window, chunks, qkv_ref, g_ref, col_ref, row_ref, att_ref, grad_ref, dk_acc, dv_acc):
+def attention_kernel(step, window, qkv_ref, g_ref, col_ref, row_ref, att_ref, grad_ref, dk_acc, dv_acc):
     i = pl.program_id(1)
     scale = HD ** (-0.5)
     low = pl.multiple_of(jnp.maximum((i + 1) * step - window, 0), step)
@@ -235,9 +244,11 @@
         dk_acc[...] = jnp.zeros_like(dk_acc)
         dv_acc[...] = jnp.zeros_like(dv_acc)
 
-    q = qkv_ref[0, mine, 0:HD]
-    k = qkv_ref[0, seen, HD : 2 * HD]
-    v = qkv_ref[0, seen, 2 * HD : 3 * HD]
+    first = low // step
+    spread = range(window // step)
+    q = qkv_ref[0, :, columns_of(i, 0)]
+    k = jnp.concatenate([qkv_ref[0, :, columns_of(first + j, 1)] for j in spread], axis=0)
+    v = jnp.concatenate([qkv_ref[0, :, columns_of(first + j, 2)] for j in spread], axis=0)
     g = g_ref[0, mine, :]
     gap = (i * step - low).astype(jnp.int32)
     ahead = lax.broadcasted_iota(jnp.int32, (step, window), 1) - lax.broadcasted_iota(
@@ -253,8 +264,7 @@
     dprob = dot_f32(g, v, NT)
     delta = jnp.sum(probs_f * dprob, axis=1, keepdims=True)
     dscore = (probs_f * (dprob - delta)).astype(jnp.bfloat16)
-    place = pl.ds(pl.multiple_of((i // chunks) * step, step), step)
-    grad_ref[0, lax.rem(i, chunks), place, 0:HD] = (dot_f32(dscore, k) * scale).astype(jnp.bfloat16)
+    grad_ref[0, :, columns_of(i, 0)] = (dot_f32(dscore, k) * scale).astype(jnp.bfloat16)
     dk_acc[seen, :] += dot_f32(dscore, q, TN)
     dv_acc[seen, :] += dot_f32(probs, g, TN)
 
@@ -262,33 +272,32 @@
     def _():
         for block in range(dk_acc.shape[0] // step):
             rows = slice(block * step, (block + 1) * step)
-            chunk, at = block % chunks, (block // chunks) * step
-            spot = slice(at, at + step)
-            grad_ref[0, chunk, spot, HD : 2 * HD] = (dk_acc[rows, :] * scale).astype(jnp.bfloat16)
-            grad_ref[0, chunk, spot, 2 * HD : 3 * HD] = dv_acc[rows, :].astype(jnp.bfloat16)
-
-
-def attention(qkv, upstream, doc_ids, step, chunks):
-    heads, rows, width = qkv.shape
+            at = (3 * block + 1) * HD
+            grad_ref[0, :, at : at + HD] = (dk_acc[rows, :] * scale).astype(jnp.bfloat16)
+            grad_ref[0, :, at + HD : at + 2 * HD] = dv_acc[rows, :].astype(jnp.bfloat16)
+
+
+def attention(qkv, upstream, doc_ids, step):
+    heads, rows = upstream.shape[:2]
     window = min((SPAN + 1) * step, rows)
     whole = lambda h, i: (h, 0, 0)
     fixed = lambda h, i: (0, 0)
     return pl.pallas_call(
-        functools.partial(attention_kernel, step, window, chunks),
+        functools.partial(attention_kernel, step, window),
         out_shape=(
             jax.ShapeDtypeStruct((heads, rows, HD), jnp.bfloat16),
-            jax.ShapeDtypeStruct((heads, chunks, rows // chunks, width), jnp.bfloat16),
+            jax.ShapeDtypeStruct(qkv.shape, jnp.bfloat16),
         ),
         grid=(heads, rows // step),
         in_specs=[
-            pl.BlockSpec((1, rows, width), whole),
+            pl.BlockSpec((1,) + qkv.shape[1:], whole),
             pl.BlockSpec((1, rows, HD), whole),
             pl.BlockSpec((rows, 1), fixed),
             pl.BlockSpec((1, rows), fixed),
         ],
         out_specs=[
             pl.BlockSpec((1, rows, HD), whole),
-            pl.BlockSpec((1, chunks, rows // chunks, width), lambda h, i: (h, 0, 0, 0)),
+            pl.BlockSpec((1,) + qkv.shape[1:], whole),
         ],
         cost_estimate=cost(10 * heads * rows * window * HD, 16 * heads * rows * HD),
         scratch_shapes=[pltpu.VMEM((rows, HD), jnp.float32)] * 2,
@@ -299,18 +308,20 @@
 
 def input_kernel(pair, mods_ref, order_ref, number_ref, d_ref, w_ref, out_ref, acc):
     step = pl.program_id(0)
+    step_rows = d_ref.shape[1]
 
     @pl.when(step == 0)
     def _():
         acc[...] = jnp.zeros_like(acc)
 
     def one(n, carry):
-        first, second = block_rows(order_ref[2 * n]), block_rows(order_ref[2 * n + 1])
+        both = (order_ref[2 * n], order_ref[2 * n + 1])
+        first, second = block_rows(both[0]), block_rows(both[1])
         modality = mods_ref[order_ref[2 * n]]
         total = jnp.concatenate([acc[first, :], acc[second, :]], axis=0)
         for p in range(3):
             parts = [
-                jnp.concatenate([d_ref[h, r, p * HD : (p + 1) * HD] for r in (first, second)], axis=0)
+                jnp.concatenate([d_ref[(h, *spot_of(b, step_rows, p))] for b in both], axis=0)
                 for h in range(pair)
             ]
             total = total + dot_f32(jnp.concatenate(parts, axis=1), w_ref[modality, p], NT)
@@ -326,7 +337,8 @@
 
 
 def input_parts(grads, planes, mods, pair):
-    heads, rows, width3 = grads.shape
+    heads, step, spread = grads.shape
+    rows = step * spread // (3 * HD)
     width = planes.shape[2]
     order, number = pair_blocks(mods)
     return pl.pallas_call(
@@ -336,7 +348,7 @@
             num_scalar_prefetch=3,
             grid=(heads // pair,),
             in_specs=[
-                pl.BlockSpec((pair, rows, width3), lambda h, *_: (h, 0, 0)),
+                pl.BlockSpec((pair, step, spread), lambda h, *_: (h, 0, 0)),
                 pl.BlockSpec((2, 3, width, pair * HD), lambda h, *_: (0, 0, 0, h)),
             ],
             out_specs=pl.BlockSpec((rows, width), lambda h, *_: (0, 0)),
@@ -348,33 +360,36 @@
     )(mods, order, number, grads, planes)
 
 
-def weight_kernel(pair, x_ref, *refs):
-    d_refs, out_ref = refs[:-1], refs[-1]
-    rows = d_refs[0].shape[1]
+def weight_kernel(pair, x_ref, d_ref, out_ref):
     for p in range(3):
-        cols = slice(p * HD, (p + 1) * HD)
-        rhs = [jnp.concatenate([d[h, :, cols] for h in range(pair)], axis=1) for d in d_refs]
+        starts = range(p * HD, d_ref.shape[2], 3 * HD)
+        rhs = jnp.concatenate(
+            [
+                jnp.concatenate([d_ref[h, :, at : at + HD] for h in range(pair)], axis=1)
+                for at in starts
+            ],
+            axis=0,
+        )
         for modality in range(2):
-            total = dot_f32(x_ref[modality, :, 0:rows], rhs[0])
-            for c in range(1, len(rhs)):
-                total = total + dot_f32(x_ref[modality, :, c * rows : (c + 1) * rows], rhs[c])
-            out_ref[modality, p] = total.astype(jnp.bfloat16)
+            out_ref[modality, p] = dot_f32(x_ref[modality], rhs).astype(jnp.bfloat16)
 
 
 def weight_grads(gathered, flipped, pair):
-    heads, rows, width3 = gathered[0].shape
+    heads, step, spread = gathered.shape
     width, total_rows = flipped.shape[1:]
     return pl.pallas_call(
         functools.partial(weight_kernel, pair),
         out_shape=jax.ShapeDtypeStruct((2, 3, width, heads * HD), jnp.bfloat16),
         grid=(heads // pair,),
-        in_specs=[pl.BlockSpec((2, width, total_rows), lambda h: (0, 0, 0))]
-        + [pl.BlockSpec((pair, rows, width3), lambda h: (h, 0, 0))] * len(gathered),
+        in_specs=[
+            pl.BlockSpec((2, width, total_rows), lambda h: (0, 0, 0)),
+            pl.BlockSpec((pair, step, spread), lambda h: (h, 0, 0)),
+        ],
         out_specs=pl.BlockSpec((2, 3, width, pair * HD), lambda h: (0, 0, 0, h)),
         compiler_params=params(),
         cost_estimate=cost(12 * total_rows * width * heads * HD, 6 * total_rows * heads * HD),
         name="weight_grads",
-    )(flipped, *gathered)
+    )(flipped, gathered)
 
 
 def place_inputs(sums):
@@ -416,40 +431,31 @@
         tiled=True,
     )
     planes = jnp.transpose(weights, (1, 2, 0, 3))
-    columns, upstream = lax.optimization_barrier((columns, upstream))
     mp = lax.axis_size("mp")
     chunks = dp // mp
-    chunk_rows = total_rows // chunks
-    dp_mods = block_modality.reshape(mp, chunks, local_rows // BLOCK)
-    partial = project(columns, planes, block_modality, pair)
+    partial = project(columns, planes, block_modality, pair, local_rows)
+    spread = dp * 3 * HD
     qkv = lax.psum_scatter(
-        partial.reshape(heads * total_rows, 3 * HD), "dp", scatter_dimension=0, tiled=True
-    )
-    token_mods = jnp.broadcast_to(
-        dp_mods.transpose(1, 0, 2)[..., None], (chunks, mp, local_rows // BLOCK, BLOCK)
-    ).reshape(total_rows)
-    shuffled = columns.reshape(mp, chunks, local_rows, columns.shape[1]).transpose(1, 0, 2, 3)
-    shuffled = shuffled.reshape(total_rows, columns.shape[1])
-    mask = token_mods[None, :] == jnp.arange(2, dtype=jnp.int32)[:, None]
-    flipped = jnp.where(mask[:, None, :], shuffled.T[None], jnp.zeros((), jnp.bfloat16))
+        partial.reshape(heads * local_rows, spread), "dp", scatter_dimension=0, tiled=True
+    )
+    token_mods = jnp.broadcast_to(block_modality[:, None], (total_rows // BLOCK, BLOCK))
+    mask = token_mods.reshape(1, total_rows) == jnp.arange(2, dtype=jnp.int32)[:, None]
+    flipped = jnp.where(mask[:, None, :], columns.T[None], jnp.zeros((), jnp.bfloat16))
     qkv, flipped = lax.optimization_barrier((qkv, flipped))
-    qkv = qkv.reshape(own, total_rows, 3 * HD)
-    attended, grads = attention(qkv, upstream, doc_ids, local_rows, chunks)
-    gathered, sums = [], []
-    for c in range(chunks):
-        flat = grads[:, c].reshape(own * chunk_rows, 3 * HD)
-        whole = lax.all_gather(flat, "dp", axis=0, tiled=True)
-        gathered.append(whole.reshape(heads, chunk_rows, 3 * HD))
-    for c in range(chunks):
-        parts = input_parts(gathered[c], planes, dp_mods[:, c].reshape(-1), pair)
-        sums.append(lax.psum_scatter(parts, "mp", scatter_dimension=0, tiled=True))
+    qkv = qkv.reshape(own, local_rows, spread)
+    attended, grads = attention(qkv, upstream, doc_ids, local_rows)
+    grads = lax.optimization_barrier(grads.reshape(own * local_rows, spread))
+    gathered = lax.optimization_barrier(lax.all_gather(grads, "dp", axis=0, tiled=True))
+    gathered = gathered.reshape(heads, local_rows, spread)
+    parts = input_parts(gathered, planes, block_modality, pair)
+    summed = lax.psum_scatter(parts, "mp", scatter_dimension=0, tiled=True)
     attended = attended.reshape(own, dp, local_rows, HD).transpose(1, 0, 2, 3)
     attended = lax.all_to_all(attended, "dp", split_axis=0, concat_axis=0, tiled=True)
     attended = attended.reshape(heads, local_rows, HD)
     attended = attended.transpose(1, 0, 2).reshape(local_rows, head_width)
     by_plane = weight_grads(gathered, flipped, pair)
-    by_plane, *sums = lax.optimization_barrier((by_plane, *sums))
-    grad_tokens = place_inputs(sums)
+    by_plane, summed = lax.optimization_barrier((by_plane, summed))
+    grad_tokens = place_inputs(jnp.split(summed, chunks, axis=0))
     grad_weights = jnp.transpose(by_plane, (2, 0, 1, 3))
     return attended, grad_tokens, grad_weights
 

time: 387 us -> 358 us (0.925)
  waiting for transfers between devices: 219 us -> 206 us
  local copies, waits for them, and re-layouts: 42.6 us -> 33.2 us
  Pallas kernels: 80.5 us -> 76.1 us
    all_to_all x1, waiting for transfers between devices: 5.05 us -> 0.01 us  [by_heads(): lax.all_to_all(grad_out.reshape(local_rows, heads, HD).transpose(1, 0, 2)...]
    reduce_scatter x3 -> x2, waiting for transfers between devices: 104 us -> 99 us  [the longest x1 77.9 us: by_heads(): lax.psum_scatter(partial.reshape(heads * local_rows, spread), 'dp', scatt...]
    pallas_call x2 -> x1, Pallas kernels: 22.7 us -> 18.4 us  [input_parts(): pl.pallas_call(functools.partial(input_kernel, pair), out_shape=jax.Shape...]
    all_gather x2 -> x1, waiting for transfers between devices: 76.3 us -> 72.8 us  [by_heads(): lax.all_gather(grads, 'dp', axis=0, tiled=True)]
    unnamed x25 -> x21, local copies, waits for them, and re-layouts: 25 us -> 24.2 us
  transfers between devices with their start and end apart: 10 -> 8, of which waited for: 8 -> 6; matrix products, arithmetic and copies ran while one was open for 11% -> 10% of each run, Pallas kernels for 11% -> 5%
where the time goes in v3:
time: 358 us; the launch traced here: 356 us
  waiting for transfers between devices  206 us (58%)
  Pallas kernels  76.1 us (21%)
  local copies, waits for them, and re-layouts  33.2 us (9%)
  starting transfers between devices  18.8 us (5%)
  between operations  15.2 us (4%)
  other arithmetic  7.01 us (2%)
    reduce_scatter x1, waiting for transfers between devices, by_heads(): lax.psum_scatter(partial.reshape(heads * local_rows, spread), 'dp', scatt...  77.9 us
    all_gather x1, waiting for transfers between devices, by_heads(): lax.all_gather(grads, 'dp', axis=0, tiled=True)  72.8 us
    unnamed x21, local copies, waits for them, and re-layouts  24.2 us
    pallas_call x1, Pallas kernels, attention(): pl.pallas_call(functools.partial(attention_kernel, step, window), out_sha...  21.2 us
    reduce_scatter x1, waiting for transfers between devices, by_heads(): summed = lax.psum_scatter(parts, 'mp', scatter_dimension=0, tiled=True)  21 us
    ppermute x2, waiting for transfers between devices, place_inputs(): piece = lax.ppermute(sent, ('dp', 'mp'), route)  19.5 us
    pallas_call x1, Pallas kernels, weight_grads(): pl.pallas_call(functools.partial(weight_kernel, pair), out_shape=jax.Shap...  18.5 us
    pallas_call x1, Pallas kernels, input_parts(): pl.pallas_call(functools.partial(input_kernel, pair), out_shape=jax.Shape...  18.4 us
  transfers between devices with their start and end apart: 8, of which 6 were waited for; matrix products, arithmetic and copies ran while one was open for 10% of the time, Pallas kernels for 5%

profile of v3, /device:TPU:3, one launch (start us, length us, event | category | flops | bytes accessed | tf_op | source)
XLA Modules:
  0.0 355.9 jit_solution(12740682611581857113)
XLA Ops:
  7.2 0.0 copy-start
  7.2 0.0 copy-start.7
  7.2 3.2 copy.58
  10.4 4.6 %all-to-all-start = ((bf16[256,8,512]{2,0,1:T(8,128)(2,1)}), bf16[256,8,512]{2,0,1:T(8,128)(2,1)S(1)}, u32[]{:S(2)}, u32[]{:S(2)}) async-start(bf16[256,8,512]{2,0,1:T(8,128)(2,1)} %bitcast.41), calls=%async_computation | async-start | bytes 4194304 | tf_op jit(solution)/shard_map/all_to_all | solution.py:425
  15.0 0.6 fusion.2
  16.9 0.2 convert_reduce_fusion
  17.1 0.1 select_reduce_fusion
  17.2 0.1 reshape.70
  17.3 0.1 fusion
  17.4 0.1 reshape.71
  17.5 0.1 fusion.3
  17.5 0.1 pad_add_fusion
  17.6 0.6 reshape.72.order_ref
  18.2 7.5 %copy.57 = bf16[512,2,3,1024]{3,0,2,1:T(8,128)(2,1)} copy(bf16[512,2,3,1024]{3,1,2,0:T(2,128)(2,1)} %param.6) | data formatting | bytes 12582912 | tf_op args[1]
  25.8 14.2 %all-to-all-done = bf16[256,8,512]{2,0,1:T(8,128)(2,1)S(1)} async-done(((bf16[256,8,512]{2,0,1:T(8,128)(2,1)}), bf16[256,8,512]{2,0,1:T(8,128)(2,1)S(1)}, u32[]{:S(2)}, u32[]{:S(2)}) %all-to-all-start) | async-done | bytes 2097184 | tf_op jit(solution)/shard_map/all_to_all | solution.py:425
  40.0 1.3 copy-done.2
  41.3 18.0 %project.1 = bf16[8,256,3072]{2,1,0:T(8,128)(2,1)} custom-call(s32[16]{0:T(128)} %mods_ref.3, s32[18]{0:T(128)} %reshape.72.order_ref, s32[1]{0:T(128)} %bitcast.number_ref, bf16[2048,512]{1,0:T(8,128)(2,1)} %bitcast.39, bf16[2,3,512,1024]{3,2,1,0:T(8,128)(2,1)} %bitcast.43), custom_call_target="tpu_custom_call" | custom-call | flops 6442450944 | bytes 12582912 | tf_op jit(solution)/shard_map/project/pallas_call | solution.py:217
  59.3 0.0 reduce-scatter.3.cloned.1.call-update
  59.3 0.9 bitcast_bitcast_fusion
  60.2 5.0 %all-to-all-start.1 = ((bf16[8,256,128]{2,1,0:T(8,128)(2,1)}), bf16[8,256,128]{2,1,0:T(8,128)(2,1)S(1)}, u32[]{:S(2)}, u32[]{:S(2)}) async-start(bf16[8,256,128]{2,1,0:T(8,128)(2,1)} %bitcast_bitcast_fusion), calls=%async_computation.2 | async-start | bytes 1048576 | tf_op jit(solution)/shard_map/all_to_all | solution.py:426
  65.2 1.4 copy.47.col_ref
  66.6 0.1 broadcast_bitcast_fusion
  66.7 2.4 copy.45
  69.1 4.8 %broadcast_select_fusion.x_ref = bf16[2,512,2048]{2,1,0:T(8,128)(2,1)} fusion(pred[2,2048]{1,0:T(4,128)(4,1)S(1)} %iota_compare_fusion, bf16[512,2048]{1,0:T(8,128)(2,1)} %copy.45), kind=kLoop, calls=%fused_computation.1 | loop fusion | flops 2097152 | bytes 6295552 | tf_op jit(solution)/shard_map/jit(_where)/select_n | solution.py:443
  73.9 77.9 %reduce-scatter.3.cloned.1.call-done = bf16[256,3072]{1,0:T(8,128)(2,1)} async-done(((bf16[2048,3072]{1,0:T(8,128)(2,1)}), bf16[256,3072]{1,0:T(8,128)(2,1)}) %reduce-scatter.3.cloned.1.call-update) | async-done | bytes 1572880 | tf_op jit(solution)/shard_map/reduce_scatter | solution.py:438
  151.8 0.0 all-to-all-done.1
  151.9 0.8 copy-done.5
  152.6 21.2 %attention.1 = (bf16[1,2048,128]{2,1,0:T(8,128)(2,1)}, bf16[1,256,3072]{2,1,0:T(8,128)(2,1)}) custom-call(bf16[1,256,3072]{2,1,0:T(8,128)(2,1)} %bitcast.53, bf16[1,2048,128]{2,1,0:T(8,128)(2,1)} %bitcast.48, s32[2048,1]{1,0:T(8,128)} %copy.47.col_ref, s32[1,2048]{1,0:T(1,128)} %bitcast.49), custom_call_target="tpu_custom_call" | custom-call | flops 3355443200 | bytes 4194304 | tf_op jit(solution)/shard_map/attention/pallas_call | solution.py:285
  173.9 0.0 all-gather.2.cloned.1.call-update
  173.9 0.0 reduce-scatter.5.cloned.1.call-start
  173.9 72.8 %all-gather.2.cloned.1.call-done = bf16[2048,3072]{1,0:T(8,128)(2,1)} async-done(((bf16[256,3072]{1,0:T(8,128)(2,1)}), bf16[2048,3072]{1,0:T(8,128)(2,1)}) %all-gather.2.cloned.1.call-update) | async-done | bytes 12582928 | tf_op jit(solution)/shard_map/all_gather | solution.py:448
  246.7 18.4 %input_parts.1 = bf16[2048,512]{1,0:T(8,128)(2,1)} custom-call(s32[16]{0:T(128)} %mods_ref.3, s32[18]{0:T(128)} %reshape.72.order_ref, s32[1]{0:T(128)} %bitcast.number_ref, bf16[8,256,3072]{2,1,0:T(8,128)(2,1)} %bitcast.51, bf16[2,3,512,1024]{3,2,1,0:T(8,128)(2,1)} %bitcast.44), custom_call_target="tpu_custom_call" | custom-call | flops 6442450944 | bytes 12582912 | tf_op jit(solution)/shard_map/input_parts/pallas_call | solution.py:344
  265.1 0.0 reduce-scatter.5.cloned.1.call-update
  265.2 3.9 %all-to-all-start.2 = ((bf16[8,1,256,128]{3,2,1,0:T(8,128)(2,1)}), bf16[8,1,256,128]{3,2,1,0:T(8,128)(2,1)S(1)}, u32[]{:S(2)}, u32[]{:S(2)}) async-start(bf16[8,1,256,128]{3,2,1,0:T(8,128)(2,1)} %bitcast.14), calls=%async_computation.3 | async-start | bytes 1048576 | tf_op jit(solution)/shard_map/all_to_all | solution.py:453
  269.0 18.5 %weight_grads.1 = bf16[2,3,512,1024]{3,2,1,0:T(8,128)(2,1)} custom-call(bf16[2,512,2048]{2,1,0:T(8,128)(2,1)} %broadcast_select_fusion.x_ref, bf16[8,256,3072]{2,1,0:T(8,128)(2,1)} %bitcast.52), custom_call_target="tpu_custom_call" | custom-call | flops 12884901888 | bytes 12582912 | tf_op jit(solution)/shard_map/weight_grads/pallas_call | solution.py:380
  287.5 21.0 %reduce-scatter.5.cloned.1.call-done = bf16[512,512]{1,0:T(8,128)(2,1)} async-done(((bf16[2048,512]{1,0:T(8,128)(2,1)}), bf16[512,512]{1,0:T(8,128)(2,1)}) %reduce-scatter.5.cloned.1.call-update) | async-done | bytes 524304 | tf_op jit(solution)/shard_map/reduce_scatter | solution.py:451
  308.6 1.1 broadcast_select_fusion.1
  309.7 1.9 collective-permute-start
  311.6 3.5 collective-permute-start.1
  315.0 0.0 all-to-all-done.2
  315.0 0.2 copy.49
  315.3 1.0 copy.50
  316.3 12.7 %copy.51 = bf16[512,2,3,1024]{3,1,2,0:T(2,128)(2,1)} copy(bf16[512,2,3,1024]{3,0,2,1:T(8,128)(2,1)} %bitcast.42) | data formatting | bytes 12582912
  329.0 13.2 %collective-permute-done = bf16[256,512]{1,0:T(8,128)(2,1)S(1)} collective-permute-done((bf16[256,512]{1,0:T(8,128)(2,1)S(1)}, bf16[256,512]{1,0:T(8,128)(2,1)S(1)}, u32[]{:S(2)}, u32[]{:S(2)}) %collective-permute-start) | collective-permute-done | bytes 262176 | tf_op jit(solution)/shard_map/ppermute | solution.py:411
  342.2 0.1 broadcast_in_dim.81
  342.3 6.3 %collective-permute-done.1 = bf16[256,512]{1,0:T(8,128)(2,1)S(1)} collective-permute-done((bf16[256,512]{1,0:T(8,128)(2,1)S(1)}, bf16[256,512]{1,0:T(8,128)(2,1)S(1)}, u32[]{:S(2)}, u32[]{:S(2)}) %collective-permute-start.1) | collective-permute-done | bytes 262176 | tf_op jit(solution)/shard_map/ppermute | solution.py:411
  348.6 0.0 copy-start.4
  348.6 0.8 copy-done.4
  (18 shorter events, 0.1 us)
Async XLA Ops:
  7.2 52.2 %copy-start = (bf16[256,1024]{1,0:T(8,128)(2,1)S(1)}, bf16[256,1024]{1,0:T(8,128)(2,1)}, u32[]{:S(2)}) copy-start(bf16[256,1024]{1,0:T(8,128)(2,1)} %param.9) | copy-start | bytes 1572868
  7.2 7.8 %copy-start.7 = (s32[16]{0:T(128)S(1)}, s32[16]{0:T(128)}, u32[]{:S(2)}) copy-start(s32[16]{0:T(128)} %mods_ref.3) | copy-start | bytes 196
  10.4 29.6 %all-to-all-start = ((bf16[256,8,512]{2,0,1:T(8,128)(2,1)}), bf16[256,8,512]{2,0,1:T(8,128)(2,1)S(1)}, u32[]{:S(2)}, u32[]{:S(2)}) async-start(bf16[256,8,512]{2,0,1:T(8,128)(2,1)} %bitcast.41), calls=%async_computation | async-start | bytes 4194304 | tf_op jit(solution)/shard_map/all_to_all | solution.py:425
  14.9 136.9 %reduce-scatter.3.cloned.1.call-start = ((), (), s32[]{:S(2)}) async-start(), calls=%async_computation.5 | async-start | bytes 14155776 | tf_op jit(solution)/shard_map/reduce_scatter | solution.py:438
  40.0 1.3 copy-start.2
  59.3 5.9 %copy-start.6 = (s32[2048]{0:T(1024)S(1)}, s32[2048]{0:T(1024)}, u32[]{:S(2)}) copy-start(s32[2048]{0:T(1024)} %param.8) | copy-start | bytes 24580
  59.3 7.3 %copy-start.8 = (s32[16]{0:T(128)S(1)}, s32[16]{0:T(128)}, u32[]{:S(2)}) copy-start(s32[16]{0:T(128)} %mods_ref.3) | copy-start | bytes 196
  59.3 7.4 %copy-start.3 = (bf16[256,8,512]{2,0,1:T(8,128)(2,1)S(1)}, bf16[256,8,512]{2,0,1:T(8,128)(2,1)}, u32[]{:S(2)}) copy-start(bf16[256,8,512]{2,0,1:T(8,128)(2,1)} %copy-done.2) | copy-start | bytes 6291460
  60.2 91.6 %all-to-all-start.1 = ((bf16[8,256,128]{2,1,0:T(8,128)(2,1)}), bf16[8,256,128]{2,1,0:T(8,128)(2,1)S(1)}, u32[]{:S(2)}, u32[]{:S(2)}) async-start(bf16[8,256,128]{2,1,0:T(8,128)(2,1)} %bitcast_bitcast_fusion), calls=%async_computation.2 | async-start | bytes 1048576 | tf_op jit(solution)/shard_map/all_to_all | solution.py:426
  65.2 181.5 %all-gather.2.cloned.1.call-start = ((), (), s32[]{:S(2)}) async-start(), calls=%async_computation.6 | async-start | bytes 14155776 | tf_op jit(solution)/shard_map/all_gather | solution.py:448
  151.9 0.8 copy-start.5
  173.9 134.7 %reduce-scatter.5.cloned.1.call-start = ((), (), s32[]{:S(2)}) async-start(), calls=%async_computation.7 | async-start | bytes 2621440 | tf_op jit(solution)/shard_map/reduce_scatter | solution.py:451
  265.2 49.9 %all-to-all-start.2 = ((bf16[8,1,256,128]{3,2,1,0:T(8,128)(2,1)}), bf16[8,1,256,128]{3,2,1,0:T(8,128)(2,1)S(1)}, u32[]{:S(2)}, u32[]{:S(2)}) async-start(bf16[8,1,256,128]{3,2,1,0:T(8,128)(2,1)} %bitcast.14), calls=%async_computation.3 | async-start | bytes 1048576 | tf_op jit(solution)/shard_map/all_to_all | solution.py:453
  309.7 32.5 %collective-permute-start = (bf16[256,512]{1,0:T(8,128)(2,1)S(1)}, bf16[256,512]{1,0:T(8,128)(2,1)S(1)}, u32[]{:S(2)}, u32[]{:S(2)}) collective-permute-start(bf16[256,512]{1,0:T(8,128)(2,1)S(1)} %get-tuple-element.31), channel_id=1, source_target_pairs={{0,0},{1,8},{2,16},{3,24},{4,4},{5,12},{6,20},{7,28},{8,1},{9,9},{... | collective-permute-start | bytes 786440 | tf_op jit(solution)/shard_map/ppermute | solution.py:411
  311.6 37.0 %collective-permute-start.1 = (bf16[256,512]{1,0:T(8,128)(2,1)S(1)}, bf16[256,512]{1,0:T(8,128)(2,1)S(1)}, u32[]{:S(2)}, u32[]{:S(2)}) collective-permute-start(bf16[256,512]{1,0:T(8,128)(2,1)S(1)} %get-tuple-element.30), channel_id=1, source_target_pairs={{0,4},{1,12},{2,20},{3,28},{4,0},{5,8},{6,16},{7,24},{8,5},{9,13},... | collective-permute-start | bytes 786440 | tf_op jit(solution)/shard_map/ppermute | solution.py:411
  316.3 33.1 %copy-start.1 = (bf16[256,1024]{1,0:T(8,128)(2,1)S(1)}, bf16[256,1024]{1,0:T(8,128)(2,1)}, u32[]{:S(2)}) copy-start(bf16[256,1024]{1,0:T(8,128)(2,1)} %param.9) | copy-start | bytes 1572868
  348.6 0.8 copy-start.4
Sparse Core Ops, SparseCore 0:
  59.4 92.3 reduce-scatter.2
  174.0 72.6 all-gather.1
  265.3 43.2 reduce-scatter.4
